TPU v7x, 256 devices: a whole 4x4x8 slice. The times are simulated.
256 devices in a mesh: seq: 64 (over z, x, core), segment: 4 (over y).
Axes of the slice: x: 4, y: 4, z: 8, core: 2. Of those that a mesh axis runs over, the one named last changes fastest.
Arguments:
- queries: bfloat16 [4, 16384, 2560], P('segment', 'seq')
- keys: bfloat16 [4, 16384, 512], P('segment', 'seq')
- values: bfloat16 [4, 16384, 512], P('segment', 'seq'), may hold values from -6 to 6
- out_proj: bfloat16 [4, 2560, 2560], P('segment', 'seq'), may hold values from -0.5 to 0.5
- hidden_in: bfloat16 [16384, 2560], P('seq'), may hold values from -3 to 3
- vertical: int32 [4, 4, 17], P('segment'), may hold values from 0 to 255, as said below
- slash: int32 [4, 4, 4], P('segment'), may hold values from 1 to 8, as said below
Outputs:
- hidden: bfloat16 [4, 16384, 2560], P('segment', 'seq')
Inputs may be any that keep to these rules, and one draw needn't show every extreme that they name: `vertical`: entry 0 of every list is block 0; each other entry lies in the blocks of a different seq index, never index 0, so one seq index holds at most one entry of a list. `slash`: the 4 offsets of one list are distinct.
All inputs are finite; a program needn't handle non-finite values.
Results may differ from a plain program's by a relative error of at most 0.006.
Values may be sent and summed in bfloat16 or wider, within the bound.
A program may use at most 320 MiB of HBM per device.

v0:
```python
import math

import jax
import jax.numpy as jnp
from jax import lax
from jax.sharding import PartitionSpec as P

HEAD = 128
BLK = 64
NS = 4


def passed_along(block, axis, distance):
    devices = range(lax.axis_size(axis))
    route = [(i - distance, i) for i in devices if i - distance in devices]
    return lax.ppermute(block, axis, route)


def pick_rows(source, index_list):
    return jnp.take(source, index_list, axis=0)


def on_device(queries, keys, values, out_proj, hidden_in, vertical, slash):
    query_rows = queries[0]
    key_rows = keys[0]
    value_rows = values[0]
    weight_rows = out_proj[0]
    vertical_list = vertical[0]
    slash_list = slash[0]
    row_count = query_rows.shape[0]
    kv_heads = key_rows.shape[1] // HEAD
    group_size = query_rows.shape[1] // HEAD // kv_heads
    block_count = row_count // BLK
    column_count = vertical_list.shape[1]
    seq_index = lax.axis_index("seq")
    scale = 1.0 / math.sqrt(HEAD)
    earlier = []
    for distance in (2, 1):
        earlier.append(passed_along((key_rows, value_rows), "seq", distance))
    ext_keys = jnp.concatenate([earlier[0][0], earlier[1][0], key_rows], axis=0)
    ext_keys = ext_keys.reshape(3 * block_count, BLK, kv_heads, HEAD)
    ext_values = jnp.concatenate([earlier[0][1], earlier[1][1], value_rows], axis=0)
    ext_values = ext_values.reshape(3 * block_count, BLK, kv_heads, HEAD)
    joined = jnp.concatenate([ext_keys, ext_values], axis=-1).transpose(2, 0, 1, 3)
    own_blocks = joined[:, 2 * block_count :]
    offsets = jnp.concatenate([jnp.zeros((kv_heads, 1), jnp.int32), slash_list], axis=1)
    local_block = jnp.arange(block_count, dtype=jnp.int32)
    global_block = seq_index * block_count + local_block
    tile_index = 2 * block_count + local_block[None, :, None] - offsets[:, None, :]
    tile_valid = global_block[None, :, None] - offsets[:, None, :] >= 0
    owner = vertical_list // block_count
    within = vertical_list - owner * block_count
    mine = owner == seq_index
    has_entry = jnp.any(mine, axis=1)
    slot_block = jnp.sum(jnp.where(mine, within, 0), axis=1)
    sending = jax.vmap(pick_rows)(own_blocks, slot_block)
    sending = jnp.where(has_entry[:, None, None], sending, jnp.zeros_like(sending))
    gathered = lax.all_gather(sending, "seq", axis=0, tiled=True)
    flat_slot = owner * kv_heads + jnp.arange(kv_heads, dtype=jnp.int32)[:, None]
    fetched = jnp.take(gathered, flat_slot.reshape(-1), axis=0).reshape(kv_heads, -1, BLK, 2 * HEAD)
    column_valid = jnp.logical_and(
        vertical_list[:, None, :] < global_block[None, :, None],
        jnp.all(
            vertical_list[:, None, :, None]
            != global_block[None, :, None, None] - slash_list[:, None, None, :],
            axis=-1,
        ),
    )
    column_wide = jnp.repeat(column_valid, BLK, axis=2)
    positions = jnp.arange(BLK, dtype=jnp.int32)
    causal = positions[:, None] >= positions[None, :]
    later_tile = jnp.arange(NS + 1, dtype=jnp.int32) > 0
    tile_mask = jnp.logical_or(later_tile[:, None, None], causal[None]).transpose(1, 0, 2)
    query_blocks = query_rows.reshape(block_count, BLK, kv_heads, group_size, HEAD)
    local_width = (NS + 1) * BLK
    outputs = []
    for group_index in range(kv_heads):
        query_group = query_blocks[:, :, group_index]
        tiles = jnp.take(joined[group_index], tile_index[group_index], axis=0)
        tiles = tiles.reshape(block_count, local_width, 2 * HEAD)
        local_scores = (
            jnp.einsum(
                "bqrd,bnd->brqn", query_group, tiles[..., :HEAD], preferred_element_type=jnp.float32
            )
            * scale
        )
        local_mask = jnp.logical_and(tile_valid[group_index][:, None, :, None], tile_mask[None])
        local_mask = local_mask.reshape(block_count, 1, BLK, local_width)
        local_scores = jnp.where(local_mask, local_scores, -jnp.inf)
        column_data = fetched[group_index].reshape(column_count * BLK, 2 * HEAD)
        column_scores = (
            jnp.einsum(
                "bqrd,nd->brqn",
                query_group,
                column_data[:, :HEAD],
                preferred_element_type=jnp.float32,
            )
            * scale
        )
        column_scores = jnp.where(
            column_wide[group_index][:, None, None, :], column_scores, -jnp.inf
        )
        row_max = jnp.maximum(jnp.max(local_scores, axis=3), jnp.max(column_scores, axis=3))
        local_expo = jnp.exp(local_scores - row_max[..., None])
        column_expo = jnp.exp(column_scores - row_max[..., None])
        total = jnp.sum(local_expo, axis=3) + jnp.sum(column_expo, axis=3)
        numerator = jnp.einsum(
            "brqn,bnd->brqd",
            local_expo.astype(jnp.bfloat16),
            tiles[..., HEAD:],
            preferred_element_type=jnp.float32,
        )
        numerator = numerator + jnp.einsum(
            "brqn,nd->brqd",
            column_expo.astype(jnp.bfloat16),
            column_data[:, HEAD:],
            preferred_element_type=jnp.float32,
        )
        attended = (numerator / total[..., None]).astype(jnp.bfloat16)
        outputs.append(attended.transpose(0, 2, 1, 3))
    attention = jnp.stack(outputs, axis=2).reshape(row_count, kv_heads * group_size * HEAD)
    delta = jnp.dot(
        attention,
        lax.all_gather(weight_rows, "seq", axis=0, tiled=True),
        preferred_element_type=jnp.float32,
    )
    segment_index = lax.axis_index("segment")
    current = (hidden_in.astype(jnp.float32) + delta).astype(jnp.bfloat16)
    for handoff_step in range(lax.axis_size("segment") - 1):
        incoming = passed_along(current, "segment", 1)
        updated = (incoming.astype(jnp.float32) + delta).astype(jnp.bfloat16)
        current = jnp.where(segment_index == handoff_step + 1, updated, current)
    return current[None]


def solution(mesh):
    in_specs = (
        P("segment", "seq", None),
        P("segment", "seq", None),
        P("segment", "seq", None),
        P("segment", "seq", None),
        P("seq", None),
        P("segment", None, None),
        P("segment", None, None),
    )
    out_specs = P("segment", "seq", None)
    return jax.shard_map(
        on_device, mesh=mesh, in_specs=in_specs, out_specs=out_specs, check_vma=False
    )
```

profile of v0, /device:TPU:25, one launch (start us, length us, event | category | flops | bytes accessed | tf_op | source)
XLA Modules:
  0.0 329.9 jit_solution(4028010175036790666)
XLA Ops:
  6.5 3.1 collective-permute-start
  9.7 4.0 %collective-permute-start.1 = (bf16[256,512]{1,0:T(8,128)(2,1)}, bf16[256,512]{1,0:T(8,128)(2,1)S(1)}, u32[]{:S(2)}, u32[]{:S(2)}) collective-permute-start(bf16[256,512]{1,0:T(8,128)(2,1)} %bitcast.303), channel_id=1, source_target_pairs={{0,4},{4,8},{8,12},{12,16},{16,20},{20,24},{24,28},{28,32},{32,36}... | collective-permute-start | bytes 786440 | tf_op jit(solution)/shard_map/ppermute | solution.py:16
  13.6 2.8 collective-permute-start.2
  16.5 2.2 collective-permute-start.3
  18.7 0.8 select_reduce_fusion
  20.0 0.8 fusion.60
  20.8 1.0 pad_maximum_fusion.1
  22.2 2.3 collective-permute-done.2
  24.5 2.8 collective-permute-done.3
  28.6 1.4 select_select_fusion
  32.5 2.6 reshape_squeeze.15
  37.7 0.8 broadcast_and_fusion.3
  38.5 3.1 fusion.67
  44.7 1.2 copy-done.8
  46.0 1.8 fusion.74
  47.8 1.8 fusion.72
  49.6 1.8 fusion.70
  51.4 1.7 fusion.68
  53.1 64.6 %all-gather.4.cloned.1.call-done = bf16[256,64,256]{2,1,0:T(8,128)(2,1)} async-done(((bf16[4,64,256]{2,1,0:T(8,128)(2,1)}), bf16[256,64,256]{2,1,0:T(8,128)(2,1)}) %all-gather.4.cloned.1.call-update) | async-done | bytes 8388624 | tf_op jit(solution)/shard_map/all_gather | solution.py:58
  117.8 4.1 %gather_fusion = bf16[68,64,256]{2,1,0:T(8,128)(2,1)S(1)} fusion(bf16[256,64,256]{2,1,0:T(8,128)(2,1)} %all-gather.4.cloned.1.call-done, s32[1024]{0:T(1024)S(1)} %pad_clamp_fusion.3), kind=kCustom, calls=%fused_computation.4 | custom fusion | bytes 4456720 | tf_op jit(solution)/shard_map/jit(_take)/gather | solution.py:60
  122.3 0.9 copy-done.9
  123.2 1.1 fusion.75
  124.4 1.1 fusion.73
  125.5 1.1 fusion.71
  126.7 1.1 fusion.69
  128.3 0.7 fusion.22
  130.2 0.7 fusion.26
  132.0 1.3 fusion.2
  133.3 1.1 fusion.4
  134.4 1.1 fusion.6
  135.5 1.1 fusion.8
  136.5 1.2 fusion.16
  138.4 1.2 fusion.14
  140.2 1.2 fusion.12
  142.0 1.2 fusion.10
  144.0 0.9 copy.37
  144.9 2.3 reshape.290
  147.2 61.5 %all-gather.6.cloned.1.call-done = bf16[1,2560,2560]{2,1,0:T(8,128)(2,1)} async-done(((bf16[1,40,2560]{2,1,0:T(8,128)(2,1)}), bf16[1,2560,2560]{2,1,0:T(8,128)(2,1)}) %all-gather.6.cloned.1.call-update) | async-done | bytes 13107216 | tf_op jit(solution)/shard_map/all_gather | solution.py:124
  208.8 10.0 %add_convert_fusion.3 = (bf16[256,2560]{1,0:T(8,128)(2,1)}, f32[256,2560]{1,0:T(8,128)S(1)}) fusion(bf16[256,2560]{1,0:T(8,128)(2,1)} %param.13, bf16[256,2560]{1,0:T(8,128)(2,1)} %reshape.290, bf16[1,2560,2560]{2,1,0:T(8,128)(2,1)} %all-gather.6.cloned.1.call-done), kind=kOutput, calls=%fused_computation.35 | convolution fusion | flops 3357409280 | bytes 19660800 | tf_op jit(solution)/shard_map/dot_general | solution.py:122
  218.8 1.3 collective-permute-start.4
  220.1 31.0 %collective-permute-done.4 = bf16[256,2560]{1,0:T(8,128)(2,1)} collective-permute-done((bf16[256,2560]{1,0:T(8,128)(2,1)}, bf16[256,2560]{1,0:T(8,128)(2,1)}, u32[]{:S(2)}, u32[]{:S(2)}) %collective-permute-start.4) | collective-permute-done | bytes 1310752 | tf_op jit(solution)/shard_map/ppermute | solution.py:16
  251.1 3.3 fusion.30
  254.4 1.3 collective-permute-start.5
  255.7 30.1 %collective-permute-done.5 = bf16[256,2560]{1,0:T(8,128)(2,1)} collective-permute-done((bf16[256,2560]{1,0:T(8,128)(2,1)}, bf16[256,2560]{1,0:T(8,128)(2,1)}, u32[]{:S(2)}, u32[]{:S(2)}) %collective-permute-start.5) | collective-permute-done | bytes 1310752 | tf_op jit(solution)/shard_map/ppermute | solution.py:16
  285.8 3.9 %fusion.31 = bf16[256,2560]{1,0:T(8,128)(2,1)} fusion(f32[256,2560]{1,0:T(8,128)S(1)} %get-tuple-element.55, bf16[256,2560]{1,0:T(8,128)(2,1)} %collective-permute-done.5, pred[]{:T(512)S(6)} %eq.16, bf16[256,2560]{1,0:T(8,128)(2,1)} %collective-permute-done.4, pred[]{:T(512)S(6)} %eq.17, bf16[256,2560]{1,0:T(8,128)(2,1)} %param.13), kind=kLoop, calls=%fused_computation.55 | loop fusion | flops 7208960 | bytes 7864322 | tf_op jit(solution)/shard_map/jit(_where)/select_n | solution.py:132
  289.7 1.3 collective-permute-start.6
  291.0 29.2 %collective-permute-done.6 = bf16[256,2560]{1,0:T(8,128)(2,1)} collective-permute-done((bf16[256,2560]{1,0:T(8,128)(2,1)}, bf16[256,2560]{1,0:T(8,128)(2,1)}, u32[]{:S(2)}, u32[]{:S(2)}) %collective-permute-start.6) | collective-permute-done | bytes 1310752 | tf_op jit(solution)/shard_map/ppermute | solution.py:16
  320.2 2.8 fusion.33
  (149 shorter events, 15.9 us)
Async XLA Ops:
  6.5 111.2 %all-gather.4.cloned.1.call-start = ((), (), s32[]{:S(2)}) async-start(), calls=%async_computation | async-start | bytes 8519680 | tf_op jit(solution)/shard_map/all_gather | solution.py:58
  6.5 14.3 %collective-permute-start = (bf16[256,512]{1,0:T(8,128)(2,1)}, bf16[256,512]{1,0:T(8,128)(2,1)S(1)}, u32[]{:S(2)}, u32[]{:S(2)}) collective-permute-start(bf16[256,512]{1,0:T(8,128)(2,1)} %bitcast.302), channel_id=1, source_target_pairs={{0,8},{4,12},{8,16},{12,20},{16,24},{20,28},{24,32},{28,36},{32,40... | collective-permute-start | bytes 786440 | tf_op jit(solution)/shard_map/ppermute | solution.py:16
  9.7 11.2 %collective-permute-start.1 = (bf16[256,512]{1,0:T(8,128)(2,1)}, bf16[256,512]{1,0:T(8,128)(2,1)S(1)}, u32[]{:S(2)}, u32[]{:S(2)}) collective-permute-start(bf16[256,512]{1,0:T(8,128)(2,1)} %bitcast.303), channel_id=1, source_target_pairs={{0,4},{4,8},{8,12},{12,16},{16,20},{20,24},{24,28},{28,32},{32,36}... | collective-permute-start | bytes 786440 | tf_op jit(solution)/shard_map/ppermute | solution.py:16
  13.6 10.9 %collective-permute-start.2 = (bf16[256,512]{1,0:T(8,128)(2,1)}, bf16[256,512]{1,0:T(8,128)(2,1)S(1)}, u32[]{:S(2)}, u32[]{:S(2)}) collective-permute-start(bf16[256,512]{1,0:T(8,128)(2,1)} %bitcast.305), channel_id=1, source_target_pairs={{0,8},{4,12},{8,16},{12,20},{16,24},{20,28},{24,32},{28,36},{32,40... | collective-permute-start | bytes 786440 | tf_op jit(solution)/shard_map/ppermute | solution.py:16
  16.5 10.8 %collective-permute-start.3 = (bf16[256,512]{1,0:T(8,128)(2,1)}, bf16[256,512]{1,0:T(8,128)(2,1)S(1)}, u32[]{:S(2)}, u32[]{:S(2)}) collective-permute-start(bf16[256,512]{1,0:T(8,128)(2,1)} %bitcast.306), channel_id=1, source_target_pairs={{0,4},{4,8},{8,12},{12,16},{16,20},{20,24},{24,28},{28,32},{32,36}... | collective-permute-start | bytes 786440 | tf_op jit(solution)/shard_map/ppermute | solution.py:16
  21.8 5.5 %copy-start.19 = (bf16[1,256,512]{2,1,0:T(8,128)(2,1)S(1)}, bf16[1,256,512]{2,1,0:T(8,128)(2,1)}, u32[]{:S(2)}) copy-start(bf16[1,256,512]{2,1,0:T(8,128)(2,1)} %param.11) | copy-start | bytes 786436
  27.7 3.1 copy-start.23
  27.8 3.2 copy-start.24
  28.0 4.5 %copy-start.10 = (bf16[1,256,2560]{2,1,0:T(8,128)(2,1)S(1)}, bf16[1,256,2560]{2,1,0:T(8,128)(2,1)}, u32[]{:S(2)}) copy-start(bf16[1,256,2560]{2,1,0:T(8,128)(2,1)} %param.9) | copy-start | bytes 3932164
  30.0 178.7 %all-gather.6.cloned.1.call-start = ((), (), s32[]{:S(2)}) async-start(), calls=%async_computation.1 | async-start | bytes 13312000 | tf_op jit(solution)/shard_map/all_gather | solution.py:124
  43.0 1.2 copy-start.27
  43.0 1.2 copy-start.28
  43.6 0.9 copy-start.25
  43.6 0.9 copy-start.26
  44.4 3.3 %copy-start.17 = (bf16[4,5,64,256]{3,2,1,0:T(8,128)(2,1)}, bf16[4,5,64,256]{3,2,1,0:T(8,128)(2,1)S(1)}, u32[]{:S(2)}) copy-start(bf16[4,5,64,256]{3,2,1,0:T(8,128)(2,1)S(1)} %get-tuple-element.59) | copy-start | bytes 1966084
  44.4 3.3 %copy-start.15 = (bf16[4,5,64,256]{3,2,1,0:T(8,128)(2,1)}, bf16[4,5,64,256]{3,2,1,0:T(8,128)(2,1)S(1)}, u32[]{:S(2)}) copy-start(bf16[4,5,64,256]{3,2,1,0:T(8,128)(2,1)S(1)} %get-tuple-element.58) | copy-start | bytes 1966084
  44.4 1.4 copy-start.8
  44.5 1.5 copy-start.22
  44.7 4.9 %copy-start.13 = (bf16[4,5,64,256]{3,2,1,0:T(8,128)(2,1)}, bf16[4,5,64,256]{3,2,1,0:T(8,128)(2,1)S(1)}, u32[]{:S(2)}) copy-start(bf16[4,5,64,256]{3,2,1,0:T(8,128)(2,1)S(1)} %get-tuple-element.57) | copy-start | bytes 1966084
  44.7 6.7 %copy-start.11 = (bf16[4,5,64,256]{3,2,1,0:T(8,128)(2,1)}, bf16[4,5,64,256]{3,2,1,0:T(8,128)(2,1)S(1)}, u32[]{:S(2)}) copy-start(bf16[4,5,64,256]{3,2,1,0:T(8,128)(2,1)S(1)} %get-tuple-element.56) | copy-start | bytes 1966084
  44.7 3.1 copy-start.6
  44.7 3.1 copy-start.21
  47.8 1.8 copy-start.5
  47.8 1.8 copy-start.20
  49.6 1.8 copy-start.4
  53.1 68.7 %copy-start.29 = (pred[68]{0:T(512)(128)(4,1)S(1)}, pred[68]{0:T(512)(128)(4,1)}, u32[]{:S(2)}) copy-start(pred[68]{0:T(512)(128)(4,1)} %compare_and_fusion.6) | copy-start | bytes 208
  122.2 1.0 copy-start.9
  123.2 1.2 copy-start.7
  126.7 1.5 copy-start.3
  127.9 1.6 copy-start.2
  128.3 2.0 copy-start.1
  129.5 1.8 copy-start
  136.5 1.2 copy-start.18
  138.4 1.2 copy-start.16
  140.2 1.2 copy-start.14
  142.0 1.2 copy-start.12
  218.8 32.3 %collective-permute-start.4 = (bf16[256,2560]{1,0:T(8,128)(2,1)}, bf16[256,2560]{1,0:T(8,128)(2,1)}, u32[]{:S(2)}, u32[]{:S(2)}) collective-permute-start(bf16[256,2560]{1,0:T(8,128)(2,1)} %get-tuple-element.54), channel_id=1, source_target_pairs={{0,1},{1,2},{2,3},{4,5},{5,6},{6,7},{8,9},{9,10},{10,11},{12,13},{... | collective-permute-start | bytes 3932168 | tf_op jit(solution)/shard_map/ppermute | solution.py:16
  254.4 31.4 %collective-permute-start.5 = (bf16[256,2560]{1,0:T(8,128)(2,1)}, bf16[256,2560]{1,0:T(8,128)(2,1)}, u32[]{:S(2)}, u32[]{:S(2)}) collective-permute-start(bf16[256,2560]{1,0:T(8,128)(2,1)} %fusion.30), channel_id=1, source_target_pairs={{0,1},{1,2},{2,3},{4,5},{5,6},{6,7},{8,9},{9,10},{10,11},{12,13},{... | collective-permute-start | bytes 3932168 | tf_op jit(solution)/shard_map/ppermute | solution.py:16
  289.7 30.5 %collective-permute-start.6 = (bf16[256,2560]{1,0:T(8,128)(2,1)}, bf16[256,2560]{1,0:T(8,128)(2,1)}, u32[]{:S(2)}, u32[]{:S(2)}) collective-permute-start(bf16[256,2560]{1,0:T(8,128)(2,1)} %fusion.31), channel_id=1, source_target_pairs={{0,1},{1,2},{2,3},{4,5},{5,6},{6,7},{8,9},{9,10},{10,11},{12,13},{... | collective-permute-start | bytes 3932168 | tf_op jit(solution)/shard_map/ppermute | solution.py:16
Sparse Core Ops, SparseCore 0:
  30.2 87.5 all-gather.3
  120.5 88.2 all-gather.5
where the time goes:
time: 333 us; the launch traced here: 330 us
  waiting for transfers between devices  222 us (67%)
  matrix products  28.8 us (9%)
  other arithmetic  25.7 us (8%)
  local copies, waits for them, and re-layouts  22.8 us (7%)
  starting transfers between devices  16 us (5%)
  between operations  14.3 us (4%)
    ppermute x7, waiting for transfers between devices, passed_along(): return lax.ppermute(block, axis, route)  95.4 us
    all_gather x1, waiting for transfers between devices, on_device(): gathered = lax.all_gather(sending, 'seq', axis=0, tiled=True)  64.6 us
    all_gather x1, waiting for transfers between devices, on_device(): lax.all_gather(weight_rows, 'seq', axis=0, tiled=True)  61.5 us
    ppermute x7, starting transfers between devices, passed_along(): return lax.ppermute(block, axis, route)  15.9 us
    dot_general x1, matrix products, on_device(): jnp.dot(attention, lax.all_gather(weight_rows, 'seq', axis=0, tiled=True)...  10 us
    reduce_sum x8, other arithmetic, on_device(): total = jnp.sum(local_expo, axis=3) + jnp.sum(column_expo, axis=3)  7.33 us
    select_n x2, other arithmetic, on_device(): current = jnp.where(segment_index == handoff_step + 1, updated, current)  7.18 us
    dot_general x4, matrix products, on_device(): jnp.einsum('bqrd,bnd->brqn', query_group, tiles[..., :HEAD], preferred_el...  7.09 us
  transfers between devices with their start and end apart: 9, of which 7 were waited for; matrix products, arithmetic and copies ran while one was open for 16% of the time, Pallas kernels for 0%

commit v1 on v0

v1 whole, which is shorter than its diff:
```python
import functools
import math

import jax
import jax.numpy as jnp
from jax import lax
from jax.experimental import pallas as pl
from jax.experimental.pallas import tpu as pltpu
from jax.sharding import PartitionSpec as P

HEAD = 128
BLK = 64
NS = 4
X_CHIPS = 4
CHUNK = 256
SUB = 128
BF16 = jnp.bfloat16
F32 = jnp.float32


def wrap(index, size):
    return lax.rem(index + size, size)


def kernel(
    x_chips, n_segment, nv, group,
    q_ref, k_ref, v_ref, w_ref, hid_ref, vert_ref, slash_ref, out_ref,
    q_buf, own, ext, slots, wbuf, wsend, wland, kall, att, yin, yout, delta,
    swap_send, swap_recv, local_sem, hid_sem, ring_send, ring_recv,
    slash_send, slash_recv, att_send, att_recv, y_send, y_recv, out_send, out_recv,
):
    seq = lax.axis_index("seq")
    seg = lax.axis_index("segment")
    chips = lax.axis_size("seq") // 2
    z_chips = chips // x_chips
    core = lax.rem(seq, 2)
    other = 1 - core
    chip = seq // 2
    z = chip // x_chips
    x = lax.rem(chip, x_chips)
    nb = k_ref.shape[0]
    rows = nb * BLK
    half = q_ref.shape[2] // 2
    kvh = k_ref.shape[2] // 2
    heads = kvh // HEAD
    vk = nv * BLK
    width = vk + (NS + 1) * BLK
    n_chunk = half // CHUNK
    wrows = w_ref.shape[0]

    def at_chip(index):
        return {"seq": index * 2 + core}

    sibling = {"seq": chip * 2 + other}
    x_plus = at_chip(z * x_chips + wrap(x + 1, x_chips))
    x_minus = at_chip(z * x_chips + wrap(x - 1, x_chips))
    z_plus = at_chip(wrap(z + 1, z_chips) * x_chips + x)
    z_minus = at_chip(wrap(z - 1, z_chips) * x_chips + x)
    next_chip = at_chip(wrap(chip + 1, chips))
    prev_chip = at_chip(wrap(chip - 1, chips))
    y_plus = {"segment": wrap(seg + 1, n_segment)}
    y_minus = {"segment": wrap(seg - 1, n_segment)}

    def remote(src, dst, send_sem, recv_sem, device):
        return pltpu.make_async_remote_copy(
            src_ref=src, dst_ref=dst, send_sem=send_sem, recv_sem=recv_sem,
            device_id=device, device_id_type=pl.DeviceIdType.MESH,
        )

    barrier = pltpu.get_barrier_semaphore()
    greeted = (sibling, x_plus, x_minus, z_plus, z_minus, next_chip, prev_chip, y_plus, y_minus)
    for device in greeted:
        pl.semaphore_signal(barrier, inc=1, device_id=device, device_id_type=pl.DeviceIdType.MESH)

    mine_kv = pl.ds(pl.multiple_of(core * kvh, 128), kvh)
    their_kv = pl.ds(pl.multiple_of(other * kvh, 128), kvh)
    mine_cols = pl.ds(pl.multiple_of(core * half, 128), half)
    their_cols = pl.ds(pl.multiple_of(other * half, 128), half)
    own_blocks = pl.ds(core * nb, nb)

    w_theirs = w_ref[:, their_cols].astype(F32)
    pad = wsend.shape[0] - wrows
    if pad:
        w_theirs = jnp.concatenate([w_theirs, jnp.zeros((pad, half), F32)], axis=0)
    wsend[...] = w_theirs.astype(BF16)

    pl.semaphore_wait(barrier, len(greeted))

    pairs = [
        (k_ref.at[:, :, their_kv], k_ref.at[:, :, mine_kv], own.at[own_blocks, :, pl.ds(0, kvh)]),
        (v_ref.at[:, :, their_kv], v_ref.at[:, :, mine_kv], own.at[own_blocks, :, pl.ds(kvh, kvh)]),
        (q_ref.at[:, :, their_cols], q_ref.at[:, :, mine_cols], q_buf.at[own_blocks]),
    ]
    swaps = [
        remote(src, dst, swap_send.at[i], swap_recv.at[i], sibling)
        for i, (src, _, dst) in enumerate(pairs)
    ]
    locals_ = [
        pltpu.make_async_copy(src, dst, local_sem.at[i]) for i, (_, src, dst) in enumerate(pairs)
    ]
    w_swap = remote(wsend, wland, swap_send.at[3], swap_recv.at[3], sibling)
    for i in (0, 1):
        swaps[i].start()
        locals_[i].start()
    w_swap.start()
    swaps[2].start()
    locals_[2].start()

    own_rows = pl.ds(pl.multiple_of(core * rows, 16), rows)
    their_rows = pl.ds(pl.multiple_of(other * rows, 16), rows)

    def hid_copies():
        away = remote(
            hid_ref.at[:, their_cols], yin.at[own_rows], swap_send.at[4], swap_recv.at[4], sibling
        )
        stay = pltpu.make_async_copy(hid_ref.at[:, mine_cols], yin.at[own_rows], hid_sem)
        return away, stay

    @pl.when(seg == 0)
    def _():
        away, stay = hid_copies()
        away.start()
        stay.start()

    for i in (0, 1):
        locals_[i].wait()
        swaps[i].wait()

    slash_copy = remote(own, ext.at[pl.ds(0, 2 * nb)], slash_send, slash_recv, next_chip)
    slash_copy.start()

    for hh in range(heads):
        for o in range(2):
            pick = jnp.int32(0)
            for j in range(nv):
                entry = vert_ref[core * heads + hh, j]
                pick += jnp.where(entry // nb == chip * 2 + o, lax.rem(entry, nb), 0)
            tile = o * nb + pick
            slots[hh, z, x, o, :, 0:HEAD] = own[tile, :, pl.ds(hh * HEAD, HEAD)]
            slots[hh, z, x, o, :, HEAD:] = own[tile, :, pl.ds(kvh + hh * HEAD, HEAD)]

    pending = []

    def ring(n, me, plus, minus, whole, part_of, sem, split):
        last = n // 2

        def message(d, k, part, sending):
            sign, device = ((1, plus), (-1, minus))[d]
            out_at = wrap(me - sign * (k - 1), n)
            in_at = wrap(me - sign * k, n)
            send = ring_send.at[sem, d * 8 + (k - 1) * 2 + max(part, 0)]
            recv = ring_recv.at[sem, d * 8 + (k - 1) * 2 + max(part, 0)]
            view = whole if part < 0 else functools.partial(part_of, part)
            place = view(out_at if sending else in_at)
            return remote(place, place, send, recv, device)

        waited = set()

        def arrive(d, k, part):
            if (d, k, part) not in waited:
                waited.add((d, k, part))
                message(d, k, part, False).wait_recv()

        def parts_of(d, k):
            order = [0, 1] if d == 0 else [1, 0]
            if k == last:
                return order[:1]
            return order if split else [-1]

        for k in range(1, last + 1):
            for d in range(2):
                for part in parts_of(d, k):
                    if k > 1:
                        arrive(d, k - 1, part if split else -1)
                    outgoing = message(d, k, part, True)
                    outgoing.start()
                    pending.append(outgoing)
            yield
        for k in range(1, last + 1):
            for d in range(2):
                for part in parts_of(d, k):
                    arrive(d, k, part)

    def x_then_z(buf, half_of, sem):
        yield from ring(
            x_chips, x, x_plus, x_minus,
            lambda p: buf.at[z, p], lambda h, p: half_of(buf.at[z, p], h), sem, False,
        )
        yield from ring(
            z_chips, z, z_plus, z_minus,
            lambda p: buf.at[p],
            lambda h, p: buf.at[p, pl.ds(h * (x_chips // 2), x_chips // 2)], sem + 1, True,
        )

    def z_then_x(buf, half_of, sem):
        yield from ring(
            z_chips, z, z_plus, z_minus,
            lambda p: buf.at[p, x], lambda h, p: half_of(buf.at[p, x], h), sem, False,
        )
        yield from ring(
            x_chips, x, x_plus, x_minus,
            lambda p: buf.at[:, p],
            lambda h, p: buf.at[pl.ds(h * (z_chips // 2), z_chips // 2), p], sem + 1, True,
        )

    def slot_half(view, h):
        return view.at[h]

    def w_half(view, h):
        return view.at[:, pl.ds(h * (CHUNK // 2), CHUNK // 2)]

    def step(generator, count=1):
        for _ in range(count):
            if next(generator, "end") == "end":
                return False
        return True

    slot_gathers = [x_then_z(slots.at[0], slot_half, 0), z_then_x(slots.at[1], slot_half, 2)]
    for generator in slot_gathers:
        step(generator)

    ext[pl.ds(2 * nb, 2 * nb)] = own[...]
    w_swap.wait()
    w_mine = w_ref[:, mine_cols].astype(F32)
    w_landed = wland[...].astype(F32)[:wrows]
    top = jnp.where(core == 0, w_mine, w_landed)
    bottom = jnp.where(core == 0, w_landed, w_mine)
    w_chip = jnp.concatenate([top, bottom], axis=0).astype(BF16)
    for ch in range(n_chunk):
        wbuf[ch, z, x] = w_chip[:, ch * CHUNK : (ch + 1) * CHUNK]

    w_gathers = [
        (z_then_x if ch % 2 == 0 else x_then_z)(wbuf.at[ch], w_half, 4 + 2 * ch)
        for ch in range(n_chunk)
    ]
    live = list(slot_gathers)
    while live:
        live = [g for g in live if step(g)]
    slash_copy.wait()
    locals_[2].wait()
    swaps[2].wait()

    lane = lax.broadcasted_iota(jnp.int32, (1, width), 1)
    diag_at = vk // 128 * 128
    shift = vk - diag_at
    tile_row = lax.broadcasted_iota(jnp.int32, (group * BLK, 128), 0) % BLK
    tile_col = lax.broadcasted_iota(jnp.int32, (group * BLK, 128), 1) - shift
    future = jnp.logical_and(
        jnp.logical_and(tile_col >= 0, tile_col < BLK), tile_col > tile_row
    )
    scale = math.log2(math.e) / math.sqrt(HEAD)

    def fetch_listed(hh):
        head = core * heads + hh
        for j in range(nv):
            entry = vert_ref[head, j]
            owner = entry // nb
            owner_chip = owner // 2
            kall[hh, pl.ds(j * BLK, BLK), :] = slots[
                hh, owner_chip // x_chips, lax.rem(owner_chip, x_chips), lax.rem(owner, 2)
            ]

    def key_info(hh):
        head = core * heads + hh
        info = jnp.zeros((1, width), jnp.int32)
        for j in range(nv):
            info = jnp.where(lane // BLK == j, vert_ref[head, j], info)
        for i in range(NS):
            info = jnp.where(lane // BLK == nv + 1 + i, slash_ref[head, i], info)
        return info

    def attend(hh, info, b):
        head = core * heads + hh
        block = chip * (2 * nb) + b
        offsets = [slash_ref[head, i] for i in range(NS)]
        for i in range(NS + 1):
            tile = 2 * nb + b - (0 if i == 0 else offsets[i - 1])
            place = pl.ds(vk + i * BLK, BLK)
            kall[hh, place, 0:HEAD] = ext[tile, :, pl.ds(hh * HEAD, HEAD)]
            kall[hh, place, HEAD:] = ext[tile, :, pl.ds(kvh + hh * HEAD, HEAD)]
        query = jnp.concatenate(
            [q_buf[b, :, pl.ds((hh * group + h) * HEAD, HEAD)] for h in range(group)], axis=0
        )
        listed = info < block
        for i in range(NS):
            listed = jnp.logical_and(listed, info != block - offsets[i])
        valid = jnp.logical_or(
            jnp.logical_and(lane < vk, listed), jnp.logical_and(lane >= vk, info <= block)
        )
        bias = jnp.where(valid, 0.0, -jnp.inf).astype(F32)
        scores = lax.dot_general(
            query, kall[hh, :, 0:HEAD], (((1,), (1,)), ((), ())), preferred_element_type=F32
        )
        scores = scores + bias
        diag = jnp.where(future, -jnp.inf, scores[:, diag_at : diag_at + 128])
        scores = jnp.concatenate(
            [scores[:, :diag_at], diag, scores[:, diag_at + 128 :]], axis=1
        )
        row_max = jnp.max(scores, axis=1, keepdims=True)
        expo = jnp.exp2((scores - row_max) * scale)
        total = jnp.sum(expo, axis=1, keepdims=True)
        numerator = jnp.dot(expo.astype(BF16), kall[hh, :, HEAD:], preferred_element_type=F32)
        result = (numerator / total).astype(BF16)
        for h in range(group):
            att[core, b, :, pl.ds((hh * group + h) * HEAD, HEAD)] = result[h * BLK : (h + 1) * BLK]

    parts = 4
    per_part = 2 * nb // parts
    att_copies = []
    live = list(w_gathers)
    for g in live:
        step(g)
    for hh in range(heads):
        fetch_listed(hh)
        info = key_info(hh)
        for part in range(parts):
            live = [g for g in live if step(g)]

            @pl.loop(part * per_part, (part + 1) * per_part)
            def _(b):
                attend(hh, info, b)

            view = att.at[
                core, pl.ds(part * per_part, per_part), :, pl.ds(hh * group * HEAD, group * HEAD)
            ]
            copy = remote(
                view, view, att_send.at[hh * parts + part], att_recv.at[hh * parts + part], sibling
            )
            copy.start()
            att_copies.append(copy)
    while live:
        live = [g for g in live if step(g)]
    for copy in att_copies:
        copy.wait()

    @pl.when(seg == 0)
    def _():
        away, stay = hid_copies()
        away.wait()
        stay.wait()

    subs = 2 * rows // SUB

    def y_copy(ch, r):
        place = (pl.ds(r * SUB, SUB), pl.ds(ch * CHUNK, CHUNK))
        return remote(
            yout.at[place], yin.at[place], y_send.at[ch * subs + r], y_recv.at[ch * subs + r], y_plus
        )

    def out_copies(ch):
        cols = pl.ds(ch * CHUNK, CHUNK)
        to = pl.ds(pl.multiple_of(core * half + ch * CHUNK, 128), CHUNK)
        stay = pltpu.make_async_copy(yout.at[own_rows, cols], out_ref.at[:, to], local_sem.at[3 + ch])
        away = remote(
            yout.at[their_rows, cols], out_ref.at[:, to], out_send.at[ch], out_recv.at[ch], sibling
        )
        return stay, away

    k_half = half
    for ch in range(n_chunk):
        left = wbuf[ch, 0 : z_chips // 2].reshape(k_half, CHUNK)
        right = wbuf[ch, z_chips // 2 :].reshape(k_half, CHUNK)
        delta[...] = jnp.dot(
            att[0].reshape(2 * rows, half), left, preferred_element_type=F32
        ) + jnp.dot(att[1].reshape(2 * rows, half), right, preferred_element_type=F32)
        for r in range(subs):
            @pl.when(seg > 0)
            def _():
                y_copy(ch, r).wait_recv()

            place = (pl.ds(r * SUB, SUB), pl.ds(ch * CHUNK, CHUNK))
            yout[place] = (yin[place].astype(F32) + delta[pl.ds(r * SUB, SUB), :]).astype(BF16)

            @pl.when(seg < n_segment - 1)
            def _():
                y_copy(ch, r).start()

        for copy in out_copies(ch):
            copy.start()

    for ch in range(n_chunk):
        for copy in out_copies(ch):
            copy.wait()

    @pl.when(seg < n_segment - 1)
    def _():
        for ch in range(n_chunk):
            for r in range(subs):
                y_copy(ch, r).wait_send()

    for copy in pending:
        copy.wait_send()


def on_device(x_chips, n_segment, queries, keys, values, out_proj, hidden_in, vertical, slash):
    row_count = queries.shape[1]
    nb = row_count // BLK
    dq = queries.shape[2]
    dkv = keys.shape[2]
    nv = vertical.shape[2]
    group = dq // dkv
    half = dq // 2
    kvh = dkv // 2
    heads = kvh // HEAD
    wrows = out_proj.shape[1]
    chips = lax.axis_size("seq") // 2
    z_chips = chips // x_chips
    n_chunk = half // CHUNK
    subs = 2 * row_count // SUB
    wpad = (wrows + 15) // 16 * 16
    width = (nv + NS + 1) * BLK
    dma = pltpu.SemaphoreType.DMA
    any_space = pl.BlockSpec(memory_space=pl.ANY)
    smem = pl.BlockSpec(memory_space=pltpu.SMEM)
    vmem = pl.BlockSpec(memory_space=pltpu.VMEM)
    out = pl.pallas_call(
        functools.partial(kernel, x_chips, n_segment, nv, group),
        out_shape=jax.ShapeDtypeStruct((row_count, dq), BF16),
        in_specs=[any_space, any_space, any_space, vmem, any_space, smem, smem],
        out_specs=any_space,
        scratch_shapes=[
            pltpu.VMEM((2 * nb, BLK, half), BF16),
            pltpu.VMEM((2 * nb, BLK, 2 * kvh), BF16),
            pltpu.VMEM((4 * nb, BLK, 2 * kvh), BF16),
            pltpu.VMEM((heads, z_chips, x_chips, 2, BLK, 2 * HEAD), BF16),
            pltpu.VMEM((n_chunk, z_chips, x_chips, 2 * wrows, CHUNK), BF16),
            pltpu.VMEM((wpad, half), BF16),
            pltpu.VMEM((wpad, half), BF16),
            pltpu.VMEM((heads, width, 2 * HEAD), BF16),
            pltpu.VMEM((2, 2 * nb, BLK, half), BF16),
            pltpu.VMEM((2 * row_count, half), BF16),
            pltpu.VMEM((2 * row_count, half), BF16),
            pltpu.VMEM((2 * row_count, CHUNK), F32),
            dma((5,)),
            dma((5,)),
            dma((3 + n_chunk,)),
            dma,
            dma((4 + 2 * n_chunk, 16)),
            dma((4 + 2 * n_chunk, 16)),
            dma,
            dma,
            dma((heads * 4,)),
            dma((heads * 4,)),
            dma((n_chunk * subs,)),
            dma((n_chunk * subs,)),
            dma((n_chunk,)),
            dma((n_chunk,)),
        ],
        compiler_params=pltpu.CompilerParams(
            collective_id=0, has_side_effects=True, vmem_limit_bytes=56 * 1024 * 1024
        ),
        name="fused_layer",
    )(
        queries[0].reshape(nb, BLK, dq),
        keys[0].reshape(nb, BLK, dkv),
        values[0].reshape(nb, BLK, dkv),
        out_proj[0],
        hidden_in,
        vertical[0],
        slash[0],
    )
    return out[None]


def solution(mesh, x_chips=X_CHIPS):
    in_specs = (
        P("segment", "seq", None),
        P("segment", "seq", None),
        P("segment", "seq", None),
        P("segment", "seq", None),
        P("seq", None),
        P("segment", None, None),
        P("segment", None, None),
    )
    out_specs = P("segment", "seq", None)
    body = functools.partial(on_device, x_chips, mesh.shape["segment"])
    return jax.shard_map(body, mesh=mesh, in_specs=in_specs, out_specs=out_specs, check_vma=False)
```

time: 333 us -> 165 us (0.50); the launches traced: 330 us -> 165 us
  waiting for transfers between devices: 222 us -> 0 us
  Pallas kernels: 0 us -> 163 us
  matrix products: 28.8 us -> 0 us
  other arithmetic: 25.7 us -> 0 us
  local copies, waits for them, and re-layouts: 22.8 us -> 2.46 us
  starting transfers between devices: 16 us -> 0 us
  between operations: 14.3 us -> 0.01 us
    pallas_call x0 -> x1, Pallas kernels: none -> 163 us  [on_device(): pl.pallas_call(functools.partial(kernel, x_chips, n_segment, nv, group),...]
    all_gather x2 -> x0, waiting for transfers between devices: 126 us -> none  [the longest x1 64.6 us: on_device(): gathered = lax.all_gather(sending, 'seq', axis=0, tiled=True)]
    ppermute x7 -> x0, waiting for transfers between devices: 95.4 us -> none  [passed_along(): return lax.ppermute(block, axis, route)]
    dot_general x17 -> x0, matrix products: 28.8 us -> none  [the longest x1 10 us: on_device(): jnp.dot(attention, lax.all_gather(weight_rows, 'seq', axis=0, tiled=True)...]
    ppermute x7 -> x0, starting transfers between devices: 15.9 us -> none  [passed_along(): return lax.ppermute(block, axis, route)]
    select_n x8 -> x0, other arithmetic: 9.24 us -> none  [the longest x2 7.18 us: on_device(): current = jnp.where(segment_index == handoff_step + 1, updated, current)]
    reduce_sum x9 -> x0, other arithmetic: 8.13 us -> none  [the longest x8 7.33 us: on_device(): total = jnp.sum(local_expo, axis=3) + jnp.sum(column_expo, axis=3)]
    gather x6 -> x0, local copies, waits for them, and re-layouts: 7 us -> none  [the longest x1 4.09 us: on_device(): jnp.take(gathered, flat_slot.reshape(-1), axis=0)]
  transfers between devices with their start and end apart: 9 -> 0, of which waited for: 7 -> 0; matrix products, arithmetic and copies ran while one was open for 16% -> 0% of each run, Pallas kernels for 0% -> 0%
where the time goes in v1:
time: 165 us
  Pallas kernels  163 us (99%)
  local copies, waits for them, and re-layouts  2.46 us (1%)
    pallas_call x1, Pallas kernels, on_device(): pl.pallas_call(functools.partial(kernel, x_chips, n_segment, nv, group),...  163 us

profile of v1, /device:TPU:25, one launch (start us, length us, event | category | flops | bytes accessed | tf_op | source)
XLA Modules:
  0.0 165.3 jit_solution(17714415863084963221)
XLA Ops:
  0.0 162.8 %fused_layer.1 = bf16[256,2560]{1,0:T(8,128)(2,1)} custom-call(bf16[4,64,2560]{2,1,0:T(8,128)(2,1)} %bitcast.8, bf16[4,64,512]{2,1,0:T(8,128)(2,1)} %bitcast.9, bf16[4,64,512]{2,1,0:T(8,128)(2,1)} %bitcast.10, bf16[40,2560]{1,0:T(8,128)(2,1)} %bitcast.11, bf16[256,2560]{1,0:T(8,128)(2,1)} %hid_ref.1, s32[4,17]{1,0:T(4,128)} %bitcast.12, s32[4,4]{1,0:T(4,128)} %bitcast.13), custom_call_target="tpu_custom_call" | custom-call | tf_op jit(solution)/shard_map/fused_layer/pallas_call | solution.py:416
  162.8 2.5 %copy.9 = bf16[1,256,2560]{2,1,0:T(8,128)(2,1)} copy(bf16[1,256,2560]{2,1,0:T(8,128)(2,1)} %bitcast.7) | data formatting | bytes 2621440

commit v2 on v1

--- a/solution.py
+++ b/solution.py
@@ -25,9 +25,9 @@
 def kernel(
     x_chips, n_segment, nv, group,
     q_ref, k_ref, v_ref, w_ref, hid_ref, vert_ref, slash_ref, out_ref,
-    q_buf, own, ext, slots, wbuf, wsend, wland, kall, att, yin, yout, delta,
-    swap_send, swap_recv, local_sem, hid_sem, ring_send, ring_recv,
-    slash_send, slash_recv, att_send, att_recv, y_send, y_recv, out_send, out_recv,
+    q_buf, k_own, v_own, picked, own, ext, row_slots, cand_out, cand_in, home_a, home_b, first_blk, wbuf, wsend, wland, kall, att, yin, yout, delta,
+    swap_send, swap_recv, local_sem, hid_sem, ring_send, ring_recv, post_send, post_recv,
+    slash_send, slash_recv, first_send, first_recv, att_send, att_recv, y_send, y_recv, out_send, out_recv,
 ):
     seq = lax.axis_index("seq")
     seg = lax.axis_index("segment")
@@ -68,7 +68,12 @@
         )
 
     barrier = pltpu.get_barrier_semaphore()
-    greeted = (sibling, x_plus, x_minus, z_plus, z_minus, next_chip, prev_chip, y_plus, y_minus)
+    z_peers = [at_chip(wrap(z + d, z_chips) * x_chips + x) for d in range(1, z_chips)]
+    x_peers = [at_chip(z * x_chips + wrap(x + d, x_chips)) for d in range(1, x_chips)]
+    x_cross = [
+        {"seq": (z * x_chips + wrap(x + d, x_chips)) * 2 + other} for d in range(1, x_chips)
+    ]
+    greeted = [sibling, next_chip, prev_chip, y_plus, y_minus] + z_peers + x_peers + x_cross
     for device in greeted:
         pl.semaphore_signal(barrier, inc=1, device_id=device, device_id_type=pl.DeviceIdType.MESH)
 
@@ -77,6 +82,14 @@
     mine_cols = pl.ds(pl.multiple_of(core * half, 128), half)
     their_cols = pl.ds(pl.multiple_of(other * half, 128), half)
     own_blocks = pl.ds(core * nb, nb)
+    own_rows = pl.ds(pl.multiple_of(core * rows, 16), rows)
+    their_rows = pl.ds(pl.multiple_of(other * rows, 16), rows)
+
+    k_load = pltpu.make_async_copy(k_ref, k_own, local_sem.at[0])
+    v_load = pltpu.make_async_copy(v_ref, v_own, local_sem.at[1])
+    q_load = pltpu.make_async_copy(q_ref.at[:, :, mine_cols], q_buf.at[own_blocks], local_sem.at[2])
+    for copy in (k_load, v_load, q_load):
+        copy.start()
 
     w_theirs = w_ref[:, their_cols].astype(F32)
     pad = wsend.shape[0] - wrows
@@ -84,30 +97,47 @@
         w_theirs = jnp.concatenate([w_theirs, jnp.zeros((pad, half), F32)], axis=0)
     wsend[...] = w_theirs.astype(BF16)
 
+    k_load.wait()
+    v_load.wait()
+    for head in range(2 * heads):
+        pick = jnp.int32(0)
+        for j in range(nv):
+            entry = vert_ref[head, j]
+            pick += jnp.where(entry // nb == seq, lax.rem(entry, nb), 0)
+        picked[head // heads, head % heads, :, 0:HEAD] = k_own[pick, :, pl.ds(head * HEAD, HEAD)]
+        picked[head // heads, head % heads, :, HEAD:] = v_own[pick, :, pl.ds(head * HEAD, HEAD)]
+    row_slots[x, core] = picked[core]
+    own[own_blocks, :, pl.ds(0, kvh)] = k_own[:, :, mine_kv]
+    own[own_blocks, :, pl.ds(kvh, kvh)] = v_own[:, :, mine_kv]
+
     pl.semaphore_wait(barrier, len(greeted))
 
-    pairs = [
-        (k_ref.at[:, :, their_kv], k_ref.at[:, :, mine_kv], own.at[own_blocks, :, pl.ds(0, kvh)]),
-        (v_ref.at[:, :, their_kv], v_ref.at[:, :, mine_kv], own.at[own_blocks, :, pl.ds(kvh, kvh)]),
-        (q_ref.at[:, :, their_cols], q_ref.at[:, :, mine_cols], q_buf.at[own_blocks]),
+    pending = []
+    posted = [0]
+
+    def post(src, dst, device):
+        i = posted[0]
+        posted[0] += 1
+        copy = remote(src, dst, post_send.at[i], post_recv.at[i], device)
+        copy.start()
+        pending.append(copy)
+        return copy
+
+    def swap(i, src, dst):
+        copy = remote(src, dst, swap_send.at[i], swap_recv.at[i], sibling)
+        copy.start()
+        return copy
+
+    row_copies = [post(picked.at[other], row_slots.at[x, core], sibling)]
+    for d in range(x_chips - 1):
+        row_copies.append(post(picked.at[core], row_slots.at[x, core], x_peers[d]))
+        row_copies.append(post(picked.at[other], row_slots.at[x, core], x_cross[d]))
+    w_swap = swap(3, wsend, wland)
+    kv_swaps = [
+        swap(0, k_own.at[:, :, their_kv], own.at[own_blocks, :, pl.ds(0, kvh)]),
+        swap(1, v_own.at[:, :, their_kv], own.at[own_blocks, :, pl.ds(kvh, kvh)]),
     ]
-    swaps = [
-        remote(src, dst, swap_send.at[i], swap_recv.at[i], sibling)
-        for i, (src, _, dst) in enumerate(pairs)
-    ]
-    locals_ = [
-        pltpu.make_async_copy(src, dst, local_sem.at[i]) for i, (_, src, dst) in enumerate(pairs)
-    ]
-    w_swap = remote(wsend, wland, swap_send.at[3], swap_recv.at[3], sibling)
-    for i in (0, 1):
-        swaps[i].start()
-        locals_[i].start()
-    w_swap.start()
-    swaps[2].start()
-    locals_[2].start()
-
-    own_rows = pl.ds(pl.multiple_of(core * rows, 16), rows)
-    their_rows = pl.ds(pl.multiple_of(other * rows, 16), rows)
+    q_swap = swap(2, q_ref.at[:, :, their_cols], q_buf.at[own_blocks])
 
     def hid_copies():
         away = remote(
@@ -121,25 +151,6 @@
         away, stay = hid_copies()
         away.start()
         stay.start()
-
-    for i in (0, 1):
-        locals_[i].wait()
-        swaps[i].wait()
-
-    slash_copy = remote(own, ext.at[pl.ds(0, 2 * nb)], slash_send, slash_recv, next_chip)
-    slash_copy.start()
-
-    for hh in range(heads):
-        for o in range(2):
-            pick = jnp.int32(0)
-            for j in range(nv):
-                entry = vert_ref[core * heads + hh, j]
-                pick += jnp.where(entry // nb == chip * 2 + o, lax.rem(entry, nb), 0)
-            tile = o * nb + pick
-            slots[hh, z, x, o, :, 0:HEAD] = own[tile, :, pl.ds(hh * HEAD, HEAD)]
-            slots[hh, z, x, o, :, HEAD:] = own[tile, :, pl.ds(kvh + hh * HEAD, HEAD)]
-
-    pending = []
 
     def ring(n, me, plus, minus, whole, part_of, sem, split):
         last = n // 2
@@ -203,23 +214,12 @@
             lambda h, p: buf.at[pl.ds(h * (z_chips // 2), z_chips // 2), p], sem + 1, True,
         )
 
-    def slot_half(view, h):
-        return view.at[h]
-
     def w_half(view, h):
         return view.at[:, pl.ds(h * (CHUNK // 2), CHUNK // 2)]
 
-    def step(generator, count=1):
-        for _ in range(count):
-            if next(generator, "end") == "end":
-                return False
-        return True
-
-    slot_gathers = [x_then_z(slots.at[0], slot_half, 0), z_then_x(slots.at[1], slot_half, 2)]
-    for generator in slot_gathers:
-        step(generator)
-
-    ext[pl.ds(2 * nb, 2 * nb)] = own[...]
+    def step(*generators):
+        return [g for g in generators if next(g, "end") != "end"]
+
     w_swap.wait()
     w_mine = w_ref[:, mine_cols].astype(F32)
     w_landed = wland[...].astype(F32)[:wrows]
@@ -228,17 +228,95 @@
     w_chip = jnp.concatenate([top, bottom], axis=0).astype(BF16)
     for ch in range(n_chunk):
         wbuf[ch, z, x] = w_chip[:, ch * CHUNK : (ch + 1) * CHUNK]
-
     w_gathers = [
-        (z_then_x if ch % 2 == 0 else x_then_z)(wbuf.at[ch], w_half, 4 + 2 * ch)
-        for ch in range(n_chunk)
+        (x_then_z if ch < 2 else z_then_x)(wbuf.at[ch], w_half, 2 * ch) for ch in range(n_chunk)
     ]
-    live = list(slot_gathers)
-    while live:
-        live = [g for g in live if step(g)]
+    live_w = set(range(n_chunk))
+    w_a = [0, 1]
+    w_b = list(range(2, n_chunk))
+
+    def step_w(indices):
+        for i in indices:
+            if i in live_w and not step(w_gathers[i]):
+                live_w.discard(i)
+
+    step_w(w_b + w_a)
+    for copy in kv_swaps:
+        copy.wait()
+    ext[pl.ds(2 * nb, 2 * nb)] = own[...]
+    for copy in row_copies:
+        copy.wait_recv()
+
+    per_head = nv - 1
+    pieces = 2 * heads // x_chips
+    for zz in range(z_chips):
+        hh = zz * x_chips // per_head
+        entry = vert_ref[core * heads + hh, 1 + zz * x_chips - hh * per_head + x]
+        owner = entry // nb
+        cand_out[zz] = row_slots[lax.rem(owner // 2, x_chips), lax.rem(owner, 2), hh]
+    cand_copies = [
+        post(cand_out.at[wrap(z + d, z_chips)], cand_in.at[z], z_peers[d - 1])
+        for d in range(1, z_chips)
+    ]
+
+    def first_copy(d):
+        return remote(
+            first_blk.at[x], first_blk.at[x], first_send.at[d - 1], first_recv, z_peers[d - 1]
+        )
+
+    @pl.when(z == 0)
+    def _():
+        for i in range(pieces):
+            piece = x * pieces + i
+            cols = pl.ds(pl.multiple_of(lax.rem(piece, 2) * HEAD, 128), HEAD)
+            first_blk[x, i] = row_slots[0, 0, piece // 2, :, cols]
+        for d in range(1, z_chips):
+            first_copy(d).start()
+
+    cand_in[z] = cand_out[z]
+    slash_copy = remote(own, ext.at[pl.ds(0, 2 * nb)], slash_send, slash_recv, next_chip)
+    slash_copy.start()
+    step_w(w_b + w_a)
+    for copy in cand_copies:
+        copy.wait_recv()
+
+    home_head = chip // per_head
+    home_entry = vert_ref[core * heads + home_head, 1 + lax.rem(chip, per_head)]
+    chosen = cand_in[home_entry // (2 * nb * x_chips)]
+    cut = home_a.shape[2]
+    home_a[z, x] = chosen[:cut]
+    home_b[z, x] = chosen[cut:]
+    a_first = [post(home_a.at[z, x], home_a.at[z, x], device) for device in z_peers]
+    b_first = [post(home_b.at[z, x], home_b.at[z, x], device) for device in x_peers]
+
+    @pl.when(z > 0)
+    def _():
+        first_copy(1).wait_recv()
+
+    first_x = [post(first_blk.at[x], first_blk.at[x], device) for device in x_peers]
+    step_w(w_b + w_a)
+    for copy in b_first:
+        copy.wait_recv()
+    b_second = [post(home_b.at[z], home_b.at[z], device) for device in z_peers]
+    for copy in a_first:
+        copy.wait_recv()
+    a_second = []
+    for h in range(heads):
+        bundle = home_a.at[pl.ds(h * (z_chips // heads), z_chips // heads), x]
+        a_second += [post(bundle, bundle, device) for device in x_peers]
+    step_w(w_b)
+    for copy in first_x + b_second + a_second:
+        copy.wait_recv()
+
+    @pl.when(z == 0)
+    def _():
+        for d in range(1, z_chips):
+            first_copy(d).wait_send()
+
     slash_copy.wait()
-    locals_[2].wait()
-    swaps[2].wait()
+    q_load.wait()
+    q_swap.wait()
+    step_w(w_a + w_b)
 
     lane = lax.broadcasted_iota(jnp.int32, (1, width), 1)
     diag_at = vk // 128 * 128
@@ -251,14 +329,13 @@
     scale = math.log2(math.e) / math.sqrt(HEAD)
 
     def fetch_listed(hh):
-        head = core * heads + hh
-        for j in range(nv):
-            entry = vert_ref[head, j]
-            owner = entry // nb
-            owner_chip = owner // 2
-            kall[hh, pl.ds(j * BLK, BLK), :] = slots[
-                hh, owner_chip // x_chips, lax.rem(owner_chip, x_chips), lax.rem(owner, 2)
-            ]
+        for kv in range(2):
+            piece = 2 * hh + kv
+            kall[hh, 0:BLK, pl.ds(kv * HEAD, HEAD)] = first_blk[piece // pieces, piece % pieces]
+        for j in range(1, nv):
+            e = hh * per_head + j - 1
+            kall[hh, pl.ds(j * BLK, cut), :] = home_a[e // x_chips, e % x_chips]
+            kall[hh, pl.ds(j * BLK + cut, BLK - cut), :] = home_b[e // x_chips, e % x_chips]
 
     def key_info(hh):
         head = core * heads + hh
@@ -307,14 +384,11 @@
     parts = 4
     per_part = 2 * nb // parts
     att_copies = []
-    live = list(w_gathers)
-    for g in live:
-        step(g)
     for hh in range(heads):
         fetch_listed(hh)
         info = key_info(hh)
         for part in range(parts):
-            live = [g for g in live if step(g)]
+            step_w({2: w_a, 5: w_a, 6: w_b}.get(hh * parts + part, ()))
 
             @pl.loop(part * per_part, (part + 1) * per_part)
             def _(b):
@@ -328,8 +402,6 @@
             )
             copy.start()
             att_copies.append(copy)
-    while live:
-        live = [g for g in live if step(g)]
     for copy in att_copies:
         copy.wait()
 
@@ -358,6 +430,8 @@
 
     k_half = half
     for ch in range(n_chunk):
+        while ch in live_w:
+            step_w(range(n_chunk))
         left = wbuf[ch, 0 : z_chips // 2].reshape(k_half, CHUNK)
         right = wbuf[ch, z_chips // 2 :].reshape(k_half, CHUNK)
         delta[...] = jnp.dot(
@@ -407,6 +481,7 @@
     z_chips = chips // x_chips
     n_chunk = half // CHUNK
     subs = 2 * row_count // SUB
+    n_post = 1 + 3 * (z_chips - 1) + (4 + heads) * (x_chips - 1)
     wpad = (wrows + 15) // 16 * 16
     width = (nv + NS + 1) * BLK
     dma = pltpu.SemaphoreType.DMA
@@ -420,9 +495,17 @@
         out_specs=any_space,
         scratch_shapes=[
             pltpu.VMEM((2 * nb, BLK, half), BF16),
+            pltpu.VMEM((nb, BLK, dkv), BF16),
+            pltpu.VMEM((nb, BLK, dkv), BF16),
+            pltpu.VMEM((2, heads, BLK, 2 * HEAD), BF16),
             pltpu.VMEM((2 * nb, BLK, 2 * kvh), BF16),
             pltpu.VMEM((4 * nb, BLK, 2 * kvh), BF16),
-            pltpu.VMEM((heads, z_chips, x_chips, 2, BLK, 2 * HEAD), BF16),
+            pltpu.VMEM((x_chips, 2, heads, BLK, 2 * HEAD), BF16),
+            pltpu.VMEM((z_chips, BLK, 2 * HEAD), BF16),
+            pltpu.VMEM((z_chips, BLK, 2 * HEAD), BF16),
+            pltpu.VMEM((z_chips, x_chips, 48, 2 * HEAD), BF16),
+            pltpu.VMEM((z_chips, x_chips, 16, 2 * HEAD), BF16),
+            pltpu.VMEM((x_chips, 2 * heads // x_chips, BLK, HEAD), BF16),
             pltpu.VMEM((n_chunk, z_chips, x_chips, 2 * wrows, CHUNK), BF16),
             pltpu.VMEM((wpad, half), BF16),
             pltpu.VMEM((wpad, half), BF16),
@@ -435,9 +518,13 @@
             dma((5,)),
             dma((3 + n_chunk,)),
             dma,
-            dma((4 + 2 * n_chunk, 16)),
-            dma((4 + 2 * n_chunk, 16)),
+            dma((2 * n_chunk, 16)),
+            dma((2 * n_chunk, 16)),
+            dma((n_post,)),
+            dma((n_post,)),
             dma,
+            dma,
+            dma((z_chips - 1,)),
             dma,
             dma((heads * 4,)),
             dma((heads * 4,)),

time: 165 us -> 137 us (0.83)
  Pallas kernels: 163 us -> 134 us
    pallas_call x1, Pallas kernels: 163 us -> 134 us  [on_device(): pl.pallas_call(functools.partial(kernel, x_chips, n_segment, nv, group),...]
where the time goes in v2:
time: 137 us
  Pallas kernels  134 us (98%)
  local copies, waits for them, and re-layouts  2.46 us (2%)
    pallas_call x1, Pallas kernels, on_device(): pl.pallas_call(functools.partial(kernel, x_chips, n_segment, nv, group),...  134 us

profile of v2, /device:TPU:25, one launch (start us, length us, event | category | flops | bytes accessed | tf_op | source)
XLA Modules:
  0.0 136.7 jit_solution(8497911887947858498)
XLA Ops:
  0.0 134.2 %fused_layer.1 = bf16[256,2560]{1,0:T(8,128)(2,1)} custom-call(bf16[4,64,2560]{2,1,0:T(8,128)(2,1)} %bitcast.8, bf16[4,64,512]{2,1,0:T(8,128)(2,1)} %bitcast.9, bf16[4,64,512]{2,1,0:T(8,128)(2,1)} %bitcast.10, bf16[40,2560]{1,0:T(8,128)(2,1)} %bitcast.11, bf16[256,2560]{1,0:T(8,128)(2,1)} %hid_ref.1, s32[4,17]{1,0:T(4,128)} %bitcast.12, s32[4,4]{1,0:T(4,128)} %bitcast.13), custom_call_target="tpu_custom_call" | custom-call | tf_op jit(solution)/shard_map/fused_layer/pallas_call | solution.py:491
  134.2 2.5 %copy.9 = bf16[1,256,2560]{2,1,0:T(8,128)(2,1)} copy(bf16[1,256,2560]{2,1,0:T(8,128)(2,1)} %bitcast.7) | data formatting | bytes 2621440

commit v3 on v2

--- a/solution.py
+++ b/solution.py
@@ -14,6 +14,13 @@
 X_CHIPS = 4
 CHUNK = 256
 SUB = 128
+SCHEDULE = {
+    0: (5, 6, 7, 8, 9), 2: (0, 1, 2, 3, 4, 5, 6, 7, 8, 9), 3: (5, 6, 7, 8, 9),
+    5: (5, 6, 7, 8, 9, 0, 1), 7: (0, 1, 5), 8: (6, 2), 9: (0, 1), 10: (2, 5, 7), 11: (0, 1, 3),
+    12: (2, 6, 5, 0), 13: (3, 8, 1, 4), 14: (2, 7, 6), 15: (3, 4, 9), 16: (2, 8, 7), 17: (3, 4),
+    19: (4, 9),
+}
+LEVELS = 4
 BF16 = jnp.bfloat16
 F32 = jnp.float32
 
@@ -25,9 +32,9 @@
 def kernel(
     x_chips, n_segment, nv, group,
     q_ref, k_ref, v_ref, w_ref, hid_ref, vert_ref, slash_ref, out_ref,
-    q_buf, k_own, v_own, picked, own, ext, row_slots, cand_out, cand_in, home_a, home_b, first_blk, wbuf, wsend, wland, kall, att, yin, yout, delta,
+    q_buf, k_own, v_own, picked, own, ext, row_slots, cand_out, cand_in, home_a, home_b, first_blk, wbuf, wsend, wland, kall, att, yin, rin, yout, eout, delta,
     swap_send, swap_recv, local_sem, hid_sem, ring_send, ring_recv, post_send, post_recv,
-    slash_send, slash_recv, first_send, first_recv, att_send, att_recv, y_send, y_recv, out_send, out_recv,
+    slash_send, slash_recv, first_send, first_recv, att_send, att_recv, y_send, y_recv, r_send, r_recv, out_send, out_recv,
 ):
     seq = lax.axis_index("seq")
     seg = lax.axis_index("segment")
@@ -43,8 +50,6 @@
     half = q_ref.shape[2] // 2
     kvh = k_ref.shape[2] // 2
     heads = kvh // HEAD
-    vk = nv * BLK
-    width = vk + (NS + 1) * BLK
     n_chunk = half // CHUNK
     wrows = w_ref.shape[0]
 
@@ -192,21 +197,29 @@
                 for part in parts_of(d, k):
                     arrive(d, k, part)
 
-    def x_then_z(buf, half_of, sem):
-        yield from ring(
-            x_chips, x, x_plus, x_minus,
-            lambda p: buf.at[z, p], lambda h, p: half_of(buf.at[z, p], h), sem, False,
-        )
+    def direct(peers, view, sem):
+        copies = []
+        for i, device in enumerate(peers):
+            copy = remote(view, view, ring_send.at[sem, i], ring_recv.at[sem, i], device)
+            copy.start()
+            copies.append(copy)
+        pending.extend(copies)
+        yield
+        for copy in copies:
+            copy.wait_recv()
+
+    def x_then_z(buf, sem):
+        yield from direct(x_peers, buf.at[z, x], sem)
         yield from ring(
             z_chips, z, z_plus, z_minus,
             lambda p: buf.at[p],
             lambda h, p: buf.at[p, pl.ds(h * (x_chips // 2), x_chips // 2)], sem + 1, True,
         )
 
-    def z_then_x(buf, half_of, sem):
+    def z_then_x(buf, sem):
         yield from ring(
             z_chips, z, z_plus, z_minus,
-            lambda p: buf.at[p, x], lambda h, p: half_of(buf.at[p, x], h), sem, False,
+            lambda p: buf.at[p, x], lambda h, p: w_half(buf.at[p, x], h), sem, False,
         )
         yield from ring(
             x_chips, x, x_plus, x_minus,
@@ -215,7 +228,8 @@
         )
 
     def w_half(view, h):
-        return view.at[:, pl.ds(h * (CHUNK // 2), CHUNK // 2)]
+        upper = wrows // 16 * 16 + 16 * (wrows % 16 > 0)
+        return view.at[pl.ds(upper * h, (2 * wrows - upper) if h else upper)]
 
     def step(*generators):
         return [g for g in generators if next(g, "end") != "end"]
@@ -227,23 +241,39 @@
     bottom = jnp.where(core == 0, w_landed, w_mine)
     w_chip = jnp.concatenate([top, bottom], axis=0).astype(BF16)
     for ch in range(n_chunk):
-        wbuf[ch, z, x] = w_chip[:, ch * CHUNK : (ch + 1) * CHUNK]
+        for i in range(2):
+            start = ch * CHUNK + i * (CHUNK // 2)
+            wbuf[i, ch, z, x] = w_chip[:, start : start + CHUNK // 2]
     w_gathers = [
-        (x_then_z if ch < 2 else z_then_x)(wbuf.at[ch], w_half, 2 * ch) for ch in range(n_chunk)
+        x_then_z(wbuf.at[0, ch], 2 * ch) for ch in range(n_chunk)
+    ] + [
+        z_then_x(wbuf.at[1, ch], 2 * (n_chunk + ch)) for ch in range(n_chunk)
     ]
-    live_w = set(range(n_chunk))
-    w_a = [0, 1]
-    w_b = list(range(2, n_chunk))
-
-    def step_w(indices):
-        for i in indices:
-            if i in live_w and not step(w_gathers[i]):
-                live_w.discard(i)
-
-    step_w(w_b + w_a)
+    live_w = set(range(2 * n_chunk))
+
+    def step_one(i):
+        if i in live_w and not step(w_gathers[i]):
+            live_w.discard(i)
+
+    def step_w(point):
+        for i in SCHEDULE.get(point, ()):
+            step_one(i)
+
+    step_w(0)
     for copy in kv_swaps:
         copy.wait()
-    ext[pl.ds(2 * nb, 2 * nb)] = own[...]
+    for hh in range(heads):
+        ext[hh, pl.ds(2 * nb, 2 * nb), :, 0:HEAD] = own[:, :, pl.ds(hh * HEAD, HEAD)]
+        ext[hh, pl.ds(2 * nb, 2 * nb), :, HEAD:] = own[:, :, pl.ds(kvh + hh * HEAD, HEAD)]
+
+    def slash_copy(hh):
+        return remote(
+            ext.at[hh, pl.ds(2 * nb, 2 * nb)], ext.at[hh, pl.ds(0, 2 * nb)],
+            slash_send.at[hh], slash_recv.at[hh], next_chip,
+        )
+
+    for hh in range(heads):
+        slash_copy(hh).start()
     for copy in row_copies:
         copy.wait_recv()
 
@@ -274,9 +304,7 @@
             first_copy(d).start()
 
     cand_in[z] = cand_out[z]
-    slash_copy = remote(own, ext.at[pl.ds(0, 2 * nb)], slash_send, slash_recv, next_chip)
-    slash_copy.start()
-    step_w(w_b + w_a)
+    step_w(2)
     for copy in cand_copies:
         copy.wait_recv()
 
@@ -294,105 +322,142 @@
         first_copy(1).wait_recv()
 
     first_x = [post(first_blk.at[x], first_blk.at[x], device) for device in x_peers]
-    step_w(w_b + w_a)
+    step_w(3)
     for copy in b_first:
         copy.wait_recv()
     b_second = [post(home_b.at[z], home_b.at[z], device) for device in z_peers]
+    step_w(4)
     for copy in a_first:
         copy.wait_recv()
     a_second = []
     for h in range(heads):
         bundle = home_a.at[pl.ds(h * (z_chips // heads), z_chips // heads), x]
         a_second += [post(bundle, bundle, device) for device in x_peers]
-    step_w(w_b)
-    for copy in first_x + b_second + a_second:
+    step_w(5)
+    for copy in first_x:
         copy.wait_recv()
-
-    @pl.when(z == 0)
-    def _():
-        for d in range(1, z_chips):
-            first_copy(d).wait_send()
-
-    slash_copy.wait()
     q_load.wait()
     q_swap.wait()
-    step_w(w_a + w_b)
-
-    lane = lax.broadcasted_iota(jnp.int32, (1, width), 1)
-    diag_at = vk // 128 * 128
-    shift = vk - diag_at
-    tile_row = lax.broadcasted_iota(jnp.int32, (group * BLK, 128), 0) % BLK
-    tile_col = lax.broadcasted_iota(jnp.int32, (group * BLK, 128), 1) - shift
-    future = jnp.logical_and(
-        jnp.logical_and(tile_col >= 0, tile_col < BLK), tile_col > tile_row
-    )
+
     scale = math.log2(math.e) / math.sqrt(HEAD)
-
-    def fetch_listed(hh):
+    local = (NS + 2) * BLK
+    listed = per_head * BLK
+    local_lane = lax.broadcasted_iota(jnp.int32, (1, local), 1) // BLK
+    listed_lane = lax.broadcasted_iota(jnp.int32, (1, listed), 1) // BLK
+    tile_row = lax.broadcasted_iota(jnp.int32, (group * BLK, 2 * BLK), 0) % BLK
+    tile_col = lax.broadcasted_iota(jnp.int32, (group * BLK, 2 * BLK), 1) - BLK
+    future = tile_col > tile_row
+
+    def query_of(hh, b):
+        return jnp.concatenate(
+            [q_buf[b, :, pl.ds((hh * group + h) * HEAD, HEAD)] for h in range(group)], axis=0
+        )
+
+    def scores_of(query, keys, bias):
+        return lax.dot_general(
+            query, keys, (((1,), (1,)), ((), ())), preferred_element_type=F32
+        ) + bias
+
+    def hidden_by(valid):
+        return jnp.where(valid, 0.0, -jnp.inf).astype(F32)
+
+    def not_slash(entries, block, offsets):
+        seen = entries < block
+        for offset in offsets:
+            seen = jnp.logical_and(seen, entries != block - offset)
+        return seen
+
+    def local_info(hh):
+        head = core * heads + hh
+        info = jnp.where(local_lane == 0, vert_ref[head, 0], 0)
+        for i in range(NS):
+            info = jnp.where(local_lane == 2 + i, slash_ref[head, i], info)
+        return info
+
+    def listed_info(hh):
+        head = core * heads + hh
+        info = jnp.zeros((1, listed), jnp.int32)
+        for j in range(per_head):
+            info = jnp.where(listed_lane == j, vert_ref[head, 1 + j], info)
+        return info
+
+    def fetch_first(hh):
         for kv in range(2):
             piece = 2 * hh + kv
-            kall[hh, 0:BLK, pl.ds(kv * HEAD, HEAD)] = first_blk[piece // pieces, piece % pieces]
-        for j in range(1, nv):
-            e = hh * per_head + j - 1
-            kall[hh, pl.ds(j * BLK, cut), :] = home_a[e // x_chips, e % x_chips]
-            kall[hh, pl.ds(j * BLK + cut, BLK - cut), :] = home_b[e // x_chips, e % x_chips]
-
-    def key_info(hh):
-        head = core * heads + hh
-        info = jnp.zeros((1, width), jnp.int32)
-        for j in range(nv):
-            info = jnp.where(lane // BLK == j, vert_ref[head, j], info)
-        for i in range(NS):
-            info = jnp.where(lane // BLK == nv + 1 + i, slash_ref[head, i], info)
-        return info
-
-    def attend(hh, info, b):
+            kall[hh, pl.ds(listed, BLK), pl.ds(kv * HEAD, HEAD)] = first_blk[
+                piece // pieces, piece % pieces
+            ]
+
+    def fetch_listed(hh):
+        for j in range(per_head):
+            e = hh * per_head + j
+            kall[hh, pl.ds(j * BLK, cut), 0 : 2 * HEAD] = home_a[e // x_chips, e % x_chips]
+            kall[hh, pl.ds(j * BLK + cut, BLK - cut), 0 : 2 * HEAD] = home_b[
+                e // x_chips, e % x_chips
+            ]
+
+    def attend(hh, info_listed, info_local, b):
         head = core * heads + hh
         block = chip * (2 * nb) + b
         offsets = [slash_ref[head, i] for i in range(NS)]
         for i in range(NS + 1):
             tile = 2 * nb + b - (0 if i == 0 else offsets[i - 1])
-            place = pl.ds(vk + i * BLK, BLK)
-            kall[hh, place, 0:HEAD] = ext[tile, :, pl.ds(hh * HEAD, HEAD)]
-            kall[hh, place, HEAD:] = ext[tile, :, pl.ds(kvh + hh * HEAD, HEAD)]
-        query = jnp.concatenate(
-            [q_buf[b, :, pl.ds((hh * group + h) * HEAD, HEAD)] for h in range(group)], axis=0
-        )
-        listed = info < block
-        for i in range(NS):
-            listed = jnp.logical_and(listed, info != block - offsets[i])
-        valid = jnp.logical_or(
-            jnp.logical_and(lane < vk, listed), jnp.logical_and(lane >= vk, info <= block)
-        )
-        bias = jnp.where(valid, 0.0, -jnp.inf).astype(F32)
-        scores = lax.dot_general(
-            query, kall[hh, :, 0:HEAD], (((1,), (1,)), ((), ())), preferred_element_type=F32
-        )
-        scores = scores + bias
-        diag = jnp.where(future, -jnp.inf, scores[:, diag_at : diag_at + 128])
+            kall[hh, pl.ds(listed + (1 + i) * BLK, BLK), 0 : 2 * HEAD] = ext[hh, tile]
+        first_seen = jnp.logical_and(local_lane == 0, not_slash(info_local, block, offsets))
+        bias = jnp.concatenate(
+            [
+                hidden_by(not_slash(info_listed, block, offsets)),
+                hidden_by(
+                    jnp.logical_or(
+                        first_seen, jnp.logical_and(local_lane > 0, info_local <= block)
+                    )
+                ),
+            ],
+            axis=1,
+        )
+        scores = scores_of(query_of(hh, b), kall[hh, :, 0:HEAD], bias)
         scores = jnp.concatenate(
-            [scores[:, :diag_at], diag, scores[:, diag_at + 128 :]], axis=1
-        )
-        row_max = jnp.max(scores, axis=1, keepdims=True)
-        expo = jnp.exp2((scores - row_max) * scale)
-        total = jnp.sum(expo, axis=1, keepdims=True)
-        numerator = jnp.dot(expo.astype(BF16), kall[hh, :, HEAD:], preferred_element_type=F32)
-        result = (numerator / total).astype(BF16)
+            [
+                scores[:, :listed],
+                jnp.where(future, -jnp.inf, scores[:, listed : listed + 2 * BLK]),
+                scores[:, listed + 2 * BLK :],
+            ],
+            axis=1,
+        )
+        top = jnp.max(scores, axis=1, keepdims=True)
+        expo = jnp.exp2((scores - top) * scale).astype(BF16)
+        sums = jnp.dot(expo, kall[hh, :, HEAD:], preferred_element_type=F32)
+        result = (sums[:, :HEAD] / sums[:, HEAD:]).astype(BF16)
         for h in range(group):
             att[core, b, :, pl.ds((hh * group + h) * HEAD, HEAD)] = result[h * BLK : (h + 1) * BLK]
 
+    for hh in range(heads):
+        kall[hh, :, 2 * HEAD :] = jnp.ones((listed + local, HEAD), BF16)
+        fetch_first(hh)
+    step_w(7)
+    for copy in b_second + a_second:
+        copy.wait_recv()
+
+    @pl.when(z == 0)
+    def _():
+        for d in range(1, z_chips):
+            first_copy(d).wait_send()
+
+    step_w(8)
     parts = 4
     per_part = 2 * nb // parts
     att_copies = []
     for hh in range(heads):
+        slash_copy(hh).wait_recv()
+    for hh in range(heads):
         fetch_listed(hh)
-        info = key_info(hh)
+        infos = (listed_info(hh), local_info(hh))
         for part in range(parts):
-            step_w({2: w_a, 5: w_a, 6: w_b}.get(hh * parts + part, ()))
-
-            @pl.loop(part * per_part, (part + 1) * per_part)
+            step_w(9 + hh * parts + part)
+
+            @pl.loop(part * per_part, (part + 1) * per_part, unroll=2)
             def _(b):
-                attend(hh, info, b)
+                attend(hh, *infos, b)
 
             view = att.at[
                 core, pl.ds(part * per_part, per_part), :, pl.ds(hh * group * HEAD, group * HEAD)
@@ -402,6 +467,7 @@
             )
             copy.start()
             att_copies.append(copy)
+    step_w(17)
     for copy in att_copies:
         copy.wait()
 
@@ -413,14 +479,104 @@
 
     subs = 2 * rows // SUB
 
-    def y_copy(ch, r):
-        place = (pl.ds(r * SUB, SUB), pl.ds(ch * CHUNK, CHUNK))
-        return remote(
-            yout.at[place], yin.at[place], y_send.at[ch * subs + r], y_recv.at[ch * subs + r], y_plus
-        )
+    def piece(ch, r):
+        return (pl.ds(r * SUB, SUB), pl.ds(ch * CHUNK, CHUNK))
+
+    def up(ch, r, src):
+        at, i = piece(ch, r), ch * subs + r
+        return remote(src.at[at], yin.at[at], y_send.at[i], y_recv.at[i], y_plus)
+
+    def down(ch, r, src):
+        at, i = piece(ch, r), ch * subs + r
+        return remote(src.at[at], rin.at[at], r_send.at[i], r_recv.at[i], y_minus)
+
+    sent = [[] for _ in range(n_segment)]
+
+    def hand_on(level, ch, k):
+        def value(buf, r):
+            return buf[piece(ch, r)].astype(F32)
+
+        def own_delta(r):
+            return delta[ch, pl.ds(r * SUB, SUB), :]
+
+        def store(buf, r, result):
+            buf[piece(ch, r)] = result.astype(BF16)
+
+        def go(way, r, src):
+            way(ch, r, src).start()
+            sent[k].append((way, ch, r, src))
+
+        def come(way, r):
+            way(ch, r, yout).wait_recv()
+
+        chain, skip01, skip12, skip23 = range(4)
+        if (level, k) == (0, 0):
+            for r, way in ((skip01, down), (skip12, up), (skip23, up), (chain, up)):
+                store(yout, r, value(yin, r) + own_delta(r))
+                go(way, r, yout)
+        elif (level, k) == (0, 1):
+            for r, way in ((skip12, down), (skip01, up)):
+                store(eout, r, own_delta(r))
+                go(way, r, eout)
+        elif (level, k) == (0, 2):
+            for r, way in ((skip23, down), (skip12, up)):
+                store(eout, r, own_delta(r))
+                go(way, r, eout)
+        elif (level, k) == (1, 0):
+            come(down, skip12)
+            store(eout, skip12, value(yout, skip12) + value(rin, skip12))
+            go(down, skip12, eout)
+        elif (level, k) == (1, 1):
+            come(down, skip23)
+            store(eout, skip23, own_delta(skip23) + value(rin, skip23))
+            go(down, skip23, eout)
+            for r in (skip12, skip23, chain):
+                come(up, r)
+                store(yout, r, value(yin, r) + own_delta(r))
+                if r != skip12:
+                    go(up, r, yout)
+        elif (level, k) == (1, 2):
+            come(up, skip01)
+            store(eout, skip01, value(yin, skip01) + own_delta(skip01))
+            go(up, skip01, eout)
+        elif (level, k) == (1, 3):
+            come(down, skip01)
+            go(down, skip01, rin)
+        elif (level, k) == (2, 0):
+            come(down, skip23)
+            store(eout, skip23, value(yout, skip23) + value(rin, skip23))
+            go(down, skip23, eout)
+        elif (level, k) == (2, 2):
+            come(down, skip01)
+            go(down, skip01, rin)
+            store(
+                yout, skip01, value(rin, skip01) + value(yin, skip01) + own_delta(skip01)
+            )
+            for r in (skip23, chain):
+                come(up, r)
+                store(yout, r, value(yin, r) + own_delta(r))
+                if r == chain:
+                    go(up, r, yout)
+        elif (level, k) == (2, 3):
+            come(down, skip12)
+            go(down, skip12, rin)
+            for r in (skip01, skip12):
+                come(up, r)
+                store(yout, r, value(rin, r) + value(yin, r) + own_delta(r))
+        elif (level, k) == (3, 1):
+            come(down, skip01)
+            store(yout, skip01, value(rin, skip01) + own_delta(skip01))
+        elif (level, k) == (3, 2):
+            come(down, skip12)
+            store(yout, skip12, value(rin, skip12) + own_delta(skip12))
+        elif (level, k) == (3, 3):
+            come(down, skip23)
+            store(yout, skip23, value(rin, skip23) + own_delta(skip23))
+            come(up, chain)
+            store(yout, chain, value(yin, chain) + own_delta(chain))
 
     def out_copies(ch):
-        cols = pl.ds(ch * CHUNK, CHUNK)
+        cols = pl.ds(pl.multiple_of(ch * CHUNK, 128), CHUNK)
         to = pl.ds(pl.multiple_of(core * half + ch * CHUNK, 128), CHUNK)
         stay = pltpu.make_async_copy(yout.at[own_rows, cols], out_ref.at[:, to], local_sem.at[3 + ch])
         away = remote(
@@ -428,41 +584,48 @@
         )
         return stay, away
 
-    k_half = half
-    for ch in range(n_chunk):
-        while ch in live_w:
-            step_w(range(n_chunk))
-        left = wbuf[ch, 0 : z_chips // 2].reshape(k_half, CHUNK)
-        right = wbuf[ch, z_chips // 2 :].reshape(k_half, CHUNK)
-        delta[...] = jnp.dot(
+    def project(ch):
+        step_w(18 + ch)
+        while ch in live_w or n_chunk + ch in live_w:
+            step_one(ch)
+            step_one(n_chunk + ch)
+        left, right = (
+            jnp.concatenate(
+                [
+                    wbuf[i, ch, k * z_chips // 2 : (k + 1) * z_chips // 2].reshape(half, CHUNK // 2)
+                    for i in range(2)
+                ],
+                axis=1,
+            )
+            for k in range(2)
+        )
+        delta[ch] = jnp.dot(
             att[0].reshape(2 * rows, half), left, preferred_element_type=F32
         ) + jnp.dot(att[1].reshape(2 * rows, half), right, preferred_element_type=F32)
-        for r in range(subs):
-            @pl.when(seg > 0)
-            def _():
-                y_copy(ch, r).wait_recv()
-
-            place = (pl.ds(r * SUB, SUB), pl.ds(ch * CHUNK, CHUNK))
-            yout[place] = (yin[place].astype(F32) + delta[pl.ds(r * SUB, SUB), :]).astype(BF16)
-
-            @pl.when(seg < n_segment - 1)
-            def _():
-                y_copy(ch, r).start()
-
-        for copy in out_copies(ch):
-            copy.start()
+
+    for t in range(n_chunk + LEVELS - 1):
+        if t < n_chunk:
+            project(t)
+        for level in range(LEVELS):
+            ch = t - level
+            if 0 <= ch < n_chunk:
+                for k in range(n_segment):
+                    pl.when(seg == k)(functools.partial(hand_on, level, ch, k))
+                if level == LEVELS - 1:
+                    for copy in out_copies(ch):
+                        copy.start()
 
     for ch in range(n_chunk):
         for copy in out_copies(ch):
             copy.wait()
 
-    @pl.when(seg < n_segment - 1)
-    def _():
-        for ch in range(n_chunk):
-            for r in range(subs):
-                y_copy(ch, r).wait_send()
-
-    for copy in pending:
+    for k in range(n_segment):
+        @pl.when(seg == k)
+        def _():
+            for way, ch, r, src in sent[k]:
+                way(ch, r, src).wait_send()
+
+    for copy in pending + [slash_copy(hh) for hh in range(heads)]:
         copy.wait_send()
 
 
@@ -483,7 +646,6 @@
     subs = 2 * row_count // SUB
     n_post = 1 + 3 * (z_chips - 1) + (4 + heads) * (x_chips - 1)
     wpad = (wrows + 15) // 16 * 16
-    width = (nv + NS + 1) * BLK
     dma = pltpu.SemaphoreType.DMA
     any_space = pl.BlockSpec(memory_space=pl.ANY)
     smem = pl.BlockSpec(memory_space=pltpu.SMEM)
@@ -499,35 +661,39 @@
             pltpu.VMEM((nb, BLK, dkv), BF16),
             pltpu.VMEM((2, heads, BLK, 2 * HEAD), BF16),
             pltpu.VMEM((2 * nb, BLK, 2 * kvh), BF16),
-            pltpu.VMEM((4 * nb, BLK, 2 * kvh), BF16),
+            pltpu.VMEM((heads, 4 * nb, BLK, 2 * HEAD), BF16),
             pltpu.VMEM((x_chips, 2, heads, BLK, 2 * HEAD), BF16),
             pltpu.VMEM((z_chips, BLK, 2 * HEAD), BF16),
             pltpu.VMEM((z_chips, BLK, 2 * HEAD), BF16),
             pltpu.VMEM((z_chips, x_chips, 48, 2 * HEAD), BF16),
             pltpu.VMEM((z_chips, x_chips, 16, 2 * HEAD), BF16),
             pltpu.VMEM((x_chips, 2 * heads // x_chips, BLK, HEAD), BF16),
-            pltpu.VMEM((n_chunk, z_chips, x_chips, 2 * wrows, CHUNK), BF16),
+            pltpu.VMEM((2, n_chunk, z_chips, x_chips, 2 * wrows, CHUNK // 2), BF16),
             pltpu.VMEM((wpad, half), BF16),
             pltpu.VMEM((wpad, half), BF16),
-            pltpu.VMEM((heads, width, 2 * HEAD), BF16),
+            pltpu.VMEM((heads, (nv + NS + 1) * BLK, 3 * HEAD), BF16),
             pltpu.VMEM((2, 2 * nb, BLK, half), BF16),
             pltpu.VMEM((2 * row_count, half), BF16),
             pltpu.VMEM((2 * row_count, half), BF16),
-            pltpu.VMEM((2 * row_count, CHUNK), F32),
+            pltpu.VMEM((2 * row_count, half), BF16),
+            pltpu.VMEM((2 * row_count, half), BF16),
+            pltpu.VMEM((n_chunk, 2 * row_count, CHUNK), F32),
             dma((5,)),
             dma((5,)),
             dma((3 + n_chunk,)),
             dma,
-            dma((2 * n_chunk, 16)),
-            dma((2 * n_chunk, 16)),
+            dma((4 * n_chunk, 16)),
+            dma((4 * n_chunk, 16)),
             dma((n_post,)),
             dma((n_post,)),
-            dma,
-            dma,
+            dma((heads,)),
+            dma((heads,)),
             dma((z_chips - 1,)),
             dma,
             dma((heads * 4,)),
             dma((heads * 4,)),
+            dma((n_chunk * subs,)),
+            dma((n_chunk * subs,)),
             dma((n_chunk * subs,)),
             dma((n_chunk * subs,)),
             dma((n_chunk,)),

time: 137 us -> 120 us (0.88)
  Pallas kernels: 134 us -> 117 us
    pallas_call x1, Pallas kernels: 134 us -> 117 us  [on_device(): pl.pallas_call(functools.partial(kernel, x_chips, n_segment, nv, group),...]
where the time goes in v3:
time: 120 us
  Pallas kernels  117 us (98%)
  local copies, waits for them, and re-layouts  2.46 us (2%)
    pallas_call x1, Pallas kernels, on_device(): pl.pallas_call(functools.partial(kernel, x_chips, n_segment, nv, group),...  117 us
    unnamed x1, local copies, waits for them, and re-layouts  2.46 us

profile of v3, /device:TPU:25, one launch (start us, length us, event | category | flops | bytes accessed | tf_op | source)
XLA Modules:
  0.0 119.7 jit_solution(16300349261102132547)
XLA Ops:
  0.0 117.2 %fused_layer.1 = bf16[256,2560]{1,0:T(8,128)(2,1)} custom-call(bf16[4,64,2560]{2,1,0:T(8,128)(2,1)} %bitcast.8, bf16[4,64,512]{2,1,0:T(8,128)(2,1)} %bitcast.9, bf16[4,64,512]{2,1,0:T(8,128)(2,1)} %bitcast.10, bf16[40,2560]{1,0:T(8,128)(2,1)} %bitcast.11, bf16[256,2560]{1,0:T(8,128)(2,1)} %hid_ref.1, s32[4,17]{1,0:T(4,128)} %bitcast.12, s32[4,4]{1,0:T(4,128)} %bitcast.13), custom_call_target="tpu_custom_call" | custom-call | tf_op jit(solution)/shard_map/fused_layer/pallas_call | solution.py:653
  117.2 2.5 %copy.9 = bf16[1,256,2560]{2,1,0:T(8,128)(2,1)} copy(bf16[1,256,2560]{2,1,0:T(8,128)(2,1)} %bitcast.7) | data formatting | bytes 2621440

commit v4 on v3

--- a/solution.py
+++ b/solution.py
@@ -15,10 +15,9 @@
 CHUNK = 256
 SUB = 128
 SCHEDULE = {
-    0: (5, 6, 7, 8, 9), 2: (0, 1, 2, 3, 4, 5, 6, 7, 8, 9), 3: (5, 6, 7, 8, 9),
-    5: (5, 6, 7, 8, 9, 0, 1), 7: (0, 1, 5), 8: (6, 2), 9: (0, 1), 10: (2, 5, 7), 11: (0, 1, 3),
-    12: (2, 6, 5, 0), 13: (3, 8, 1, 4), 14: (2, 7, 6), 15: (3, 4, 9), 16: (2, 8, 7), 17: (3, 4),
-    19: (4, 9),
+    0: (11,), 2: (10, 11), 3: (11,), 5: (10, 11, 0, 1), 7: (11, 0, 1, 5), 8: (6, 2), 9: (0, 1),
+    10: (2, 5, 7), 11: (0, 1, 3), 12: (2, 6, 5, 0), 13: (3, 8, 1, 4), 14: (2, 7, 6), 15: (3, 4, 9),
+    16: (2, 8, 7), 17: (3, 4), 19: (4, 9),
 }
 LEVELS = 4
 BF16 = jnp.bfloat16
@@ -208,29 +207,6 @@
         for copy in copies:
             copy.wait_recv()
 
-    def x_then_z(buf, sem):
-        yield from direct(x_peers, buf.at[z, x], sem)
-        yield from ring(
-            z_chips, z, z_plus, z_minus,
-            lambda p: buf.at[p],
-            lambda h, p: buf.at[p, pl.ds(h * (x_chips // 2), x_chips // 2)], sem + 1, True,
-        )
-
-    def z_then_x(buf, sem):
-        yield from ring(
-            z_chips, z, z_plus, z_minus,
-            lambda p: buf.at[p, x], lambda h, p: w_half(buf.at[p, x], h), sem, False,
-        )
-        yield from ring(
-            x_chips, x, x_plus, x_minus,
-            lambda p: buf.at[:, p],
-            lambda h, p: buf.at[pl.ds(h * (z_chips // 2), z_chips // 2), p], sem + 1, True,
-        )
-
-    def w_half(view, h):
-        upper = wrows // 16 * 16 + 16 * (wrows % 16 > 0)
-        return view.at[pl.ds(upper * h, (2 * wrows - upper) if h else upper)]
-
     def step(*generators):
         return [g for g in generators if next(g, "end") != "end"]
 
@@ -243,13 +219,33 @@
     for ch in range(n_chunk):
         for i in range(2):
             start = ch * CHUNK + i * (CHUNK // 2)
-            wbuf[i, ch, z, x] = w_chip[:, start : start + CHUNK // 2]
-    w_gathers = [
-        x_then_z(wbuf.at[0, ch], 2 * ch) for ch in range(n_chunk)
-    ] + [
-        z_then_x(wbuf.at[1, ch], 2 * (n_chunk + ch)) for ch in range(n_chunk)
-    ]
-    live_w = set(range(2 * n_chunk))
+            wbuf[i, z, x, ch] = w_chip[:, start : start + CHUNK // 2]
+    x_half = x_chips // 2
+    z_half = z_chips // 2
+
+    def along_z(ch):
+        return ring(
+            z_chips, z, z_plus, z_minus, lambda p: wbuf.at[0, p, :, ch],
+            lambda h, p: wbuf.at[0, p, pl.ds(h * x_half, x_half), ch], ch, True,
+        )
+
+    def along_x(ch):
+        return ring(
+            x_chips, x, x_plus, x_minus, lambda p: wbuf.at[1, :, p, ch],
+            lambda h, p: wbuf.at[1, pl.ds(h * z_half, z_half), p, ch], n_chunk + ch, True,
+        )
+
+    upper = (n_chunk + 1) // 2
+    w_gathers = [along_z(ch) for ch in range(n_chunk)] + [along_x(ch) for ch in range(n_chunk)]
+    w_gathers.append(direct(x_peers, wbuf.at[0, z, x], 2 * n_chunk))
+    w_gathers.append(
+        ring(
+            z_chips, z, z_plus, z_minus, lambda p: wbuf.at[1, p, x],
+            lambda h, p: wbuf.at[1, p, x, pl.ds(h * upper, n_chunk - upper if h else upper)],
+            2 * n_chunk + 1, False,
+        )
+    )
+    live_w = set(range(2 * n_chunk + 2))
 
     def step_one(i):
         if i in live_w and not step(w_gathers[i]):
@@ -592,7 +588,7 @@
         left, right = (
             jnp.concatenate(
                 [
-                    wbuf[i, ch, k * z_chips // 2 : (k + 1) * z_chips // 2].reshape(half, CHUNK // 2)
+                    wbuf[i, k * z_half : (k + 1) * z_half, :, ch].reshape(half, CHUNK // 2)
                     for i in range(2)
                 ],
                 axis=1,
@@ -668,7 +664,7 @@
             pltpu.VMEM((z_chips, x_chips, 48, 2 * HEAD), BF16),
             pltpu.VMEM((z_chips, x_chips, 16, 2 * HEAD), BF16),
             pltpu.VMEM((x_chips, 2 * heads // x_chips, BLK, HEAD), BF16),
-            pltpu.VMEM((2, n_chunk, z_chips, x_chips, 2 * wrows, CHUNK // 2), BF16),
+            pltpu.VMEM((2, z_chips, x_chips, n_chunk, 2 * wrows, CHUNK // 2), BF16),
             pltpu.VMEM((wpad, half), BF16),
             pltpu.VMEM((wpad, half), BF16),
             pltpu.VMEM((heads, (nv + NS + 1) * BLK, 3 * HEAD), BF16),
@@ -682,8 +678,8 @@
             dma((5,)),
             dma((3 + n_chunk,)),
             dma,
-            dma((4 * n_chunk, 16)),
-            dma((4 * n_chunk, 16)),
+            dma((2 * n_chunk + 2, 16)),
+            dma((2 * n_chunk + 2, 16)),
             dma((n_post,)),
             dma((n_post,)),
             dma((heads,)),

time: 120 us -> 117 us (0.975)
  Pallas kernels: 117 us -> 115 us
    pallas_call x1, Pallas kernels: 117 us -> 115 us  [on_device(): pl.pallas_call(functools.partial(kernel, x_chips, n_segment, nv, group),...]
where the time goes in v4:
time: 117 us
  Pallas kernels  115 us (98%)
  local copies, waits for them, and re-layouts  2.46 us (2%)
    pallas_call x1, Pallas kernels, on_device(): pl.pallas_call(functools.partial(kernel, x_chips, n_segment, nv, group),...  115 us
    unnamed x1, local copies, waits for them, and re-layouts  2.46 us

profile of v4, /device:TPU:25, one launch (start us, length us, event | category | flops | bytes accessed | tf_op | source)
XLA Modules:
  0.0 117.3 jit_solution(14102959243309406361)
XLA Ops:
  0.0 114.8 %fused_layer.1 = bf16[256,2560]{1,0:T(8,128)(2,1)} custom-call(bf16[4,64,2560]{2,1,0:T(8,128)(2,1)} %bitcast.8, bf16[4,64,512]{2,1,0:T(8,128)(2,1)} %bitcast.9, bf16[4,64,512]{2,1,0:T(8,128)(2,1)} %bitcast.10, bf16[40,2560]{1,0:T(8,128)(2,1)} %bitcast.11, bf16[256,2560]{1,0:T(8,128)(2,1)} %hid_ref.1, s32[4,17]{1,0:T(4,128)} %bitcast.12, s32[4,4]{1,0:T(4,128)} %bitcast.13), custom_call_target="tpu_custom_call" | custom-call | tf_op jit(solution)/shard_map/fused_layer/pallas_call | solution.py:649
  114.8 2.5 %copy.9 = bf16[1,256,2560]{2,1,0:T(8,128)(2,1)} copy(bf16[1,256,2560]{2,1,0:T(8,128)(2,1)} %bitcast.7) | data formatting | bytes 2621440

commit v5 on v4

--- a/solution.py
+++ b/solution.py
@@ -31,7 +31,7 @@
 def kernel(
     x_chips, n_segment, nv, group,
     q_ref, k_ref, v_ref, w_ref, hid_ref, vert_ref, slash_ref, out_ref,
-    q_buf, k_own, v_own, picked, own, ext, row_slots, cand_out, cand_in, home_a, home_b, first_blk, wbuf, wsend, wland, kall, att, yin, rin, yout, eout, delta,
+    q_buf, k_own, v_own, picked, own, ext, row_slots, cand_out, cand_in, homes, first_blk, wbuf, wsend, wland, kall, att, yin, rin, yout, eout, delta,
     swap_send, swap_recv, local_sem, hid_sem, ring_send, ring_recv, post_send, post_recv,
     slash_send, slash_recv, first_send, first_recv, att_send, att_recv, y_send, y_recv, r_send, r_recv, out_send, out_recv,
 ):
@@ -232,7 +232,7 @@
     def along_x(ch):
         return ring(
             x_chips, x, x_plus, x_minus, lambda p: wbuf.at[1, :, p, ch],
-            lambda h, p: wbuf.at[1, pl.ds(h * z_half, z_half), p, ch], n_chunk + ch, True,
+            lambda h, p: wbuf.at[1, pl.ds(h * z_half, z_half), p, ch], n_chunk + ch, False,
         )
 
     upper = (n_chunk + 1) // 2
@@ -307,11 +307,8 @@
     home_head = chip // per_head
     home_entry = vert_ref[core * heads + home_head, 1 + lax.rem(chip, per_head)]
     chosen = cand_in[home_entry // (2 * nb * x_chips)]
-    cut = home_a.shape[2]
-    home_a[z, x] = chosen[:cut]
-    home_b[z, x] = chosen[cut:]
-    a_first = [post(home_a.at[z, x], home_a.at[z, x], device) for device in z_peers]
-    b_first = [post(home_b.at[z, x], home_b.at[z, x], device) for device in x_peers]
+    homes[z, x] = chosen
+    home_z = [post(homes.at[z, x], homes.at[z, x], device) for device in z_peers]
 
     @pl.when(z > 0)
     def _():
@@ -319,16 +316,12 @@
 
     first_x = [post(first_blk.at[x], first_blk.at[x], device) for device in x_peers]
     step_w(3)
-    for copy in b_first:
+    for copy in home_z:
         copy.wait_recv()
-    b_second = [post(home_b.at[z], home_b.at[z], device) for device in z_peers]
-    step_w(4)
-    for copy in a_first:
-        copy.wait_recv()
-    a_second = []
+    home_x = []
     for h in range(heads):
-        bundle = home_a.at[pl.ds(h * (z_chips // heads), z_chips // heads), x]
-        a_second += [post(bundle, bundle, device) for device in x_peers]
+        bundle = homes.at[pl.ds(h * (z_chips // heads), z_chips // heads), x]
+        home_x += [post(bundle, bundle, device) for device in x_peers]
     step_w(5)
     for copy in first_x:
         copy.wait_recv()
@@ -387,10 +380,7 @@
     def fetch_listed(hh):
         for j in range(per_head):
             e = hh * per_head + j
-            kall[hh, pl.ds(j * BLK, cut), 0 : 2 * HEAD] = home_a[e // x_chips, e % x_chips]
-            kall[hh, pl.ds(j * BLK + cut, BLK - cut), 0 : 2 * HEAD] = home_b[
-                e // x_chips, e % x_chips
-            ]
+            kall[hh, pl.ds(j * BLK, BLK), 0 : 2 * HEAD] = homes[e // x_chips, e % x_chips]
 
     def attend(hh, info_listed, info_local, b):
         head = core * heads + hh
@@ -431,7 +421,7 @@
         kall[hh, :, 2 * HEAD :] = jnp.ones((listed + local, HEAD), BF16)
         fetch_first(hh)
     step_w(7)
-    for copy in b_second + a_second:
+    for copy in home_x:
         copy.wait_recv()
 
     @pl.when(z == 0)
@@ -640,7 +630,7 @@
     z_chips = chips // x_chips
     n_chunk = half // CHUNK
     subs = 2 * row_count // SUB
-    n_post = 1 + 3 * (z_chips - 1) + (4 + heads) * (x_chips - 1)
+    n_post = 1 + 2 * (z_chips - 1) + (3 + heads) * (x_chips - 1)
     wpad = (wrows + 15) // 16 * 16
     dma = pltpu.SemaphoreType.DMA
     any_space = pl.BlockSpec(memory_space=pl.ANY)
@@ -661,8 +651,7 @@
             pltpu.VMEM((x_chips, 2, heads, BLK, 2 * HEAD), BF16),
             pltpu.VMEM((z_chips, BLK, 2 * HEAD), BF16),
             pltpu.VMEM((z_chips, BLK, 2 * HEAD), BF16),
-            pltpu.VMEM((z_chips, x_chips, 48, 2 * HEAD), BF16),
-            pltpu.VMEM((z_chips, x_chips, 16, 2 * HEAD), BF16),
+            pltpu.VMEM((z_chips, x_chips, BLK, 2 * HEAD), BF16),
             pltpu.VMEM((x_chips, 2 * heads // x_chips, BLK, HEAD), BF16),
             pltpu.VMEM((2, z_chips, x_chips, n_chunk, 2 * wrows, CHUNK // 2), BF16),
             pltpu.VMEM((wpad, half), BF16),

time: 117 us -> 117 us (level)
  no operation moved by 1% of the time
where the time goes in v5:
time: 117 us
  Pallas kernels  114 us (97%)
  local copies, waits for them, and re-layouts  2.46 us (2%)
    pallas_call x1, Pallas kernels, on_device(): pl.pallas_call(functools.partial(kernel, x_chips, n_segment, nv, group),...  114 us
    unnamed x1, local copies, waits for them, and re-layouts  2.46 us

profile of v5, /device:TPU:25, one launch (start us, length us, event | category | flops | bytes accessed | tf_op | source)
XLA Modules:
  0.0 116.9 jit_solution(5802080307490171546)
XLA Ops:
  0.0 114.4 %fused_layer.1 = bf16[256,2560]{1,0:T(8,128)(2,1)} custom-call(bf16[4,64,2560]{2,1,0:T(8,128)(2,1)} %bitcast.8, bf16[4,64,512]{2,1,0:T(8,128)(2,1)} %bitcast.9, bf16[4,64,512]{2,1,0:T(8,128)(2,1)} %bitcast.10, bf16[40,2560]{1,0:T(8,128)(2,1)} %bitcast.11, bf16[256,2560]{1,0:T(8,128)(2,1)} %hid_ref.1, s32[4,17]{1,0:T(4,128)} %bitcast.12, s32[4,4]{1,0:T(4,128)} %bitcast.13), custom_call_target="tpu_custom_call" | custom-call | tf_op jit(solution)/shard_map/fused_layer/pallas_call | solution.py:639
  114.4 2.5 %copy.9 = bf16[1,256,2560]{2,1,0:T(8,128)(2,1)} copy(bf16[1,256,2560]{2,1,0:T(8,128)(2,1)} %bitcast.7) | data formatting | bytes 2621440
